TPU v7x, 32 devices: a whole 2x2x4 slice. The times are simulated.
32 devices in a mesh: dp: 8 (over y, x, core), tensor: 4 (over z).
Axes of the slice: x: 2, y: 2, z: 4, core: 2. Of those that a mesh axis runs over, the one named last changes fastest.
Arguments:
- inputs: bfloat16 [2, 8, 1024, 768], P(None, 'dp'), may hold values from -6 to 6
- memory: bfloat16 [2, 8, 1024, 768], P(None, 'dp'), may hold values from -6 to 6
- cotangent: bfloat16 [2, 8, 1024, 768], P(None, 'dp', 'tensor'), may hold values from -6 to 6
- dec_len: int32 [2, 8], P(None, 'dp'), may hold values from 128 to 1024, as said below
- mem_len: int32 [2, 8], P(None, 'dp'), may hold values from 128 to 1024, as said below
- self_qkv: bfloat16 [3, 768, 768], P(None, None, 'tensor'), may hold values from -0.21875 to 0.21875
- self_out: bfloat16 [768, 768], P('tensor'), may hold values from -0.875 to 0.875
- cross_q: bfloat16 [768, 768], P(None, 'tensor'), may hold values from -0.21875 to 0.21875
- cross_kv: bfloat16 [2, 768, 768], P(None, None, 'tensor'), may hold values from -0.21875 to 0.21875
- cross_out: bfloat16 [768, 768], P('tensor'), may hold values from -0.875 to 0.875
- ffn_in: bfloat16 [768, 3072], P(None, 'tensor'), may hold values from -0.21875 to 0.21875
- ffn_out: bfloat16 [3072, 768], P('tensor'), may hold values from -0.109375 to 0.109375
- ln_gain: float32 [3, 768], replicated, may hold values from 0.5 to 1.5
- ln_bias: float32 [3, 768], replicated, may hold values from -3 to 3
Outputs:
- out: bfloat16 [2, 8, 1024, 768], P(None, 'dp', 'tensor')
- d_inputs: float32 [2, 8, 1024, 768], P(None, 'dp', 'tensor')
- d_memory: float32 [2, 8, 1024, 768], P(None, 'dp', 'tensor')
- d_self_qkv: float32 [3, 768, 768], P(None, None, 'tensor')
- d_self_out: float32 [768, 768], P('tensor')
- d_cross_q: float32 [768, 768], P(None, 'tensor')
- d_cross_kv: float32 [2, 768, 768], P(None, None, 'tensor')
- d_cross_out: float32 [768, 768], P('tensor')
- d_ffn_in: float32 [768, 3072], P(None, 'tensor')
- d_ffn_out: float32 [3072, 768], P('tensor')
- d_gain: float32 [3, 768], replicated
- d_bias: float32 [3, 768], replicated
Inputs may be any that keep to these rules, and one draw needn't show every extreme that they name: `dec_len`: in every micro-batch some sequence has all 1024 positions valid. `mem_len`: in every micro-batch some memory has all 1024 positions valid.
All inputs are finite; a program needn't handle non-finite values.
Results may differ from a plain program's by a relative error of at most 0.019.
Values may be sent and summed in bfloat16 or wider, within the bound.
No kernel may reach another device: no remote copies, remote signals or barrier semaphores. Data moves between devices by JAX's collectives and lax.ppermute only.
A program may use at most 192 MiB of HBM per device.

v0:
```python
import jax
import jax.numpy as jnp
from jax import lax
from jax.sharding import PartitionSpec as P

HEAD = 64


EPS = 1e-05


def norm_rows(resid, gain, shift):
    center = resid - jnp.mean(resid, -1, keepdims=True)
    spread = jnp.mean(center * center, -1, keepdims=True)
    return center * lax.rsqrt(spread + EPS) * gain + shift


def activate(value):
    return jax.nn.gelu(value, approximate=False)


def dot_nn(left, right):
    return jnp.dot(left, right, preferred_element_type=jnp.float32)


def dot_tn(left, right):
    return lax.dot_general(
        left, right, (((0,), (0,)), ((), ())), preferred_element_type=jnp.float32
    )


def dot_nt(left, right):
    return lax.dot_general(
        left, right, (((1,), (1,)), ((), ())), preferred_element_type=jnp.float32
    )


def split_heads(matrix):
    return matrix.reshape(matrix.shape[0], -1, HEAD)


def self_mask(first_row, row_count, key_count, length):
    query_pos = first_row + lax.broadcasted_iota(jnp.int32, (row_count, key_count), 0)
    key_pos = lax.broadcasted_iota(jnp.int32, (row_count, key_count), 1)
    return (key_pos <= query_pos) & (key_pos < length)


def cross_mask(first_row, row_count, key_count, length):
    key_pos = lax.broadcasted_iota(jnp.int32, (row_count, key_count), 1)
    return key_pos < length


def attend_forward(query, keys_in, values_in, masker, length):
    total_rows = query.shape[0]
    block_rows = min(512, total_rows)
    key_heads = split_heads(keys_in)
    value_heads = split_heads(values_in)
    factor = HEAD ** (-0.5)

    def one_block(block_index):
        first_row = block_index * block_rows
        query_heads = split_heads(lax.dynamic_slice_in_dim(query, first_row, block_rows, 0))
        scores = (
            jnp.einsum("qhd,khd->hqk", query_heads, key_heads, preferred_element_type=jnp.float32)
            * factor
        )
        scores = jnp.where(
            masker(first_row, block_rows, keys_in.shape[0], length)[None], scores, -1e30
        )
        row_peak = jnp.max(scores, -1, keepdims=True)
        exp_scores = jnp.exp(scores - row_peak)
        totals = jnp.sum(exp_scores, -1, keepdims=True)
        softmax_w = (exp_scores / totals).astype(jnp.bfloat16)
        mixed = jnp.einsum(
            "hqk,khd->qhd", softmax_w, value_heads, preferred_element_type=jnp.float32
        )
        return (
            mixed.reshape(block_rows, -1).astype(jnp.bfloat16),
            (row_peak + jnp.log(totals))[:, :, 0],
        )

    outputs, logsum = lax.map(one_block, jnp.arange(total_rows // block_rows))
    return (outputs.reshape(total_rows, -1), logsum)


def attend_backward(query, keys_in, values_in, logsum, grad_out, masker, length):
    total_rows = query.shape[0]
    block_rows = min(512, total_rows)
    key_heads = split_heads(keys_in)
    value_heads = split_heads(values_in)
    factor = HEAD ** (-0.5)

    def one_block(running, block_index):
        grad_keys, grad_values = running
        first_row = block_index * block_rows
        query_heads = split_heads(lax.dynamic_slice_in_dim(query, first_row, block_rows, 0))
        out_heads = split_heads(lax.dynamic_slice_in_dim(grad_out, first_row, block_rows, 0))
        scores = (
            jnp.einsum("qhd,khd->hqk", query_heads, key_heads, preferred_element_type=jnp.float32)
            * factor
        )
        scores = jnp.where(
            masker(first_row, block_rows, keys_in.shape[0], length)[None], scores, -1e30
        )
        softmax_w = jnp.exp(scores - logsum[block_index][:, :, None])
        grad_values = grad_values + jnp.einsum(
            "hqk,qhd->khd",
            softmax_w.astype(jnp.bfloat16),
            out_heads,
            preferred_element_type=jnp.float32,
        )
        grad_weights = jnp.einsum(
            "qhd,khd->hqk", out_heads, value_heads, preferred_element_type=jnp.float32
        )
        inner = jnp.sum(softmax_w * grad_weights, -1, keepdims=True)
        grad_scores = (softmax_w * (grad_weights - inner)).astype(jnp.bfloat16)
        grad_query = (
            jnp.einsum("hqk,khd->qhd", grad_scores, key_heads, preferred_element_type=jnp.float32)
            * factor
        )
        grad_keys = (
            grad_keys
            + jnp.einsum(
                "hqk,qhd->khd", grad_scores, query_heads, preferred_element_type=jnp.float32
            )
            * factor
        )
        return ((grad_keys, grad_values), grad_query.reshape(block_rows, -1))

    empty_heads = jnp.zeros(key_heads.shape, jnp.float32)
    (grad_keys, grad_values), grad_query = lax.scan(
        one_block, (empty_heads, empty_heads), jnp.arange(total_rows // block_rows)
    )
    key_rows = keys_in.shape[0]
    return (
        grad_query.reshape(total_rows, -1),
        grad_keys.reshape(key_rows, -1),
        grad_values.reshape(key_rows, -1),
    )


def reduce_weights(grads):
    return lax.psum((grads[0], grads[1], grads[2], grads[3], grads[4], grads[5], grads[6]), "dp")


def local(
    inputs,
    memory,
    cotangent,
    dec_len,
    mem_len,
    self_qkv,
    self_out,
    cross_q,
    cross_kv,
    cross_out,
    ffn_in,
    ffn_out,
    ln_gain,
    ln_bias,
):
    tensor_parts = lax.axis_size("tensor")
    local_rows = inputs.shape[2] // tensor_parts
    row_start = lax.axis_index("tensor") * local_rows

    def sequence(running, seq_item):
        x_full, mem_full, grad_y, dec_one, mem_one = seq_item
        x_rows = lax.dynamic_slice_in_dim(x_full, row_start, local_rows, 0).astype(jnp.float32)
        query_s = dot_nn(x_full, self_qkv[0]).astype(jnp.bfloat16)
        key_s = dot_nn(x_full, self_qkv[1]).astype(jnp.bfloat16)
        value_s = dot_nn(x_full, self_qkv[2]).astype(jnp.bfloat16)
        attn_self, logsum_self = attend_forward(query_s, key_s, value_s, self_mask, dec_one)
        branch_one = lax.psum_scatter(
            dot_nn(attn_self, self_out), "tensor", scatter_dimension=0, tiled=True
        )
        normed_one, back_one = jax.vjp(norm_rows, x_rows + branch_one, ln_gain[0], ln_bias[0])
        full_one = lax.all_gather(normed_one.astype(jnp.bfloat16), "tensor", axis=0, tiled=True)
        query_c = dot_nn(full_one, cross_q).astype(jnp.bfloat16)
        key_c = dot_nn(mem_full, cross_kv[0]).astype(jnp.bfloat16)
        value_c = dot_nn(mem_full, cross_kv[1]).astype(jnp.bfloat16)
        attn_cross, logsum_cross = attend_forward(query_c, key_c, value_c, cross_mask, mem_one)
        branch_two = lax.psum_scatter(
            dot_nn(attn_cross, cross_out), "tensor", scatter_dimension=0, tiled=True
        )
        normed_two, back_two = jax.vjp(norm_rows, normed_one + branch_two, ln_gain[1], ln_bias[1])
        full_two = lax.all_gather(normed_two.astype(jnp.bfloat16), "tensor", axis=0, tiled=True)
        hidden_pre = dot_nn(full_two, ffn_in)
        hidden_act, back_act = jax.vjp(activate, hidden_pre)
        hidden_low = hidden_act.astype(jnp.bfloat16)
        branch_three = lax.psum_scatter(
            dot_nn(hidden_low, ffn_out), "tensor", scatter_dimension=0, tiled=True
        )
        result, back_three = jax.vjp(norm_rows, normed_two + branch_three, ln_gain[2], ln_bias[2])
        grad_res3, gain_three, shift_three = back_three(grad_y.astype(jnp.float32))
        grad_b3 = lax.all_gather(grad_res3.astype(jnp.bfloat16), "tensor", axis=0, tiled=True)
        grad_act = dot_nt(grad_b3, ffn_out)
        grad_pre = back_act(grad_act)[0].astype(jnp.bfloat16)
        grad_down = dot_tn(hidden_low, grad_b3)
        grad_up = dot_tn(full_two, grad_pre)
        grad_norm2 = grad_res3 + lax.psum_scatter(
            dot_nt(grad_pre, ffn_in).astype(jnp.bfloat16), "tensor", scatter_dimension=0, tiled=True
        ).astype(jnp.float32)
        grad_res2, gain_two, shift_two = back_two(grad_norm2)
        grad_b2 = lax.all_gather(grad_res2.astype(jnp.bfloat16), "tensor", axis=0, tiled=True)
        grad_attn_c = dot_nt(grad_b2, cross_out).astype(jnp.bfloat16)
        grad_wo_cross = dot_tn(attn_cross, grad_b2)
        grad_qc, grad_kc, grad_vc = attend_backward(
            query_c, key_c, value_c, logsum_cross, grad_attn_c, cross_mask, mem_one
        )
        grad_qc = grad_qc.astype(jnp.bfloat16)
        grad_kc = grad_kc.astype(jnp.bfloat16)
        grad_vc = grad_vc.astype(jnp.bfloat16)
        grad_wq_cross = dot_tn(full_one, grad_qc)
        grad_wkv_cross = jnp.stack([dot_tn(mem_full, grad_kc), dot_tn(mem_full, grad_vc)])
        back_query, back_memory = (
            lax.psum_scatter(dot_nt(grad_qc, cross_q), "tensor", scatter_dimension=0, tiled=True),
            lax.psum_scatter(
                dot_nt(grad_kc, cross_kv[0]) + dot_nt(grad_vc, cross_kv[1]),
                "tensor",
                scatter_dimension=0,
                tiled=True,
            ),
        )
        grad_res1, gain_one, shift_one = back_one(grad_res2 + back_query)
        grad_b1 = lax.all_gather(grad_res1.astype(jnp.bfloat16), "tensor", axis=0, tiled=True)
        grad_attn_s = dot_nt(grad_b1, self_out).astype(jnp.bfloat16)
        grad_wo_self = dot_tn(attn_self, grad_b1)
        grad_qs, grad_ks, grad_vs = attend_backward(
            query_s, key_s, value_s, logsum_self, grad_attn_s, self_mask, dec_one
        )
        grad_qs = grad_qs.astype(jnp.bfloat16)
        grad_ks = grad_ks.astype(jnp.bfloat16)
        grad_vs = grad_vs.astype(jnp.bfloat16)
        grad_wqkv = jnp.stack(
            [dot_tn(x_full, grad_qs), dot_tn(x_full, grad_ks), dot_tn(x_full, grad_vs)]
        )
        part_q = dot_nt(grad_qs, self_qkv[0])
        part_k = dot_nt(grad_ks, self_qkv[1])
        part_v = dot_nt(grad_vs, self_qkv[2])
        grad_x = grad_res1 + lax.psum_scatter(
            (part_q + part_k + part_v).astype(jnp.bfloat16),
            "tensor",
            scatter_dimension=0,
            tiled=True,
        ).astype(jnp.float32)
        weights_acc, norms_acc = running
        new_weights = (
            weights_acc[0] + grad_wqkv,
            weights_acc[1] + grad_wo_self,
            weights_acc[2] + grad_wq_cross,
            weights_acc[3] + grad_wkv_cross,
            weights_acc[4] + grad_wo_cross,
            weights_acc[5] + grad_up,
            weights_acc[6] + grad_down,
        )
        new_norms = (
            norms_acc[0] + jnp.stack([gain_one, gain_two, gain_three]),
            norms_acc[1] + jnp.stack([shift_one, shift_two, shift_three]),
        )
        return ((new_weights, new_norms), (result.astype(jnp.bfloat16), grad_x, back_memory))

    weight_zero = tuple(
        (
            jnp.zeros(weight_arr.shape, jnp.float32)
            for weight_arr in (self_qkv, self_out, cross_q, cross_kv, cross_out, ffn_in, ffn_out)
        )
    )
    norm_zero = (jnp.zeros(ln_gain.shape, jnp.float32), jnp.zeros(ln_bias.shape, jnp.float32))
    seq_pieces = []
    running = (weight_zero, norm_zero)
    for micro_index in range(inputs.shape[0]):
        running, seq_outputs = lax.scan(
            sequence,
            running,
            (
                inputs[micro_index],
                memory[micro_index],
                cotangent[micro_index],
                dec_len[micro_index],
                mem_len[micro_index],
            ),
        )
        seq_pieces.append(seq_outputs)
    summed = reduce_weights(running[0])
    norms = running[1]
    norm_sums = lax.psum((norms[0], norms[1]), ("dp", "tensor"))
    result_all = jnp.stack([seq_piece[0] for seq_piece in seq_pieces])
    grad_inputs = jnp.stack([seq_piece[1] for seq_piece in seq_pieces])
    grad_memory = jnp.stack([seq_piece[2] for seq_piece in seq_pieces])
    return (
        result_all,
        grad_inputs,
        grad_memory,
        summed[0],
        summed[1],
        summed[2],
        summed[3],
        summed[4],
        summed[5],
        summed[6],
        norm_sums[0],
        norm_sums[1],
    )


def solution(mesh):
    in_specs = (
        P(None, "dp", None, None),
        P(None, "dp", None, None),
        P(None, "dp", "tensor", None),
        P(None, "dp"),
        P(None, "dp"),
        P(None, None, "tensor"),
        P("tensor", None),
        P(None, "tensor"),
        P(None, None, "tensor"),
        P("tensor", None),
        P(None, "tensor"),
        P("tensor", None),
        P(),
        P(),
    )
    out_specs = (
        P(None, "dp", "tensor", None),
        P(None, "dp", "tensor", None),
        P(None, "dp", "tensor", None),
        P(None, None, "tensor"),
        P("tensor", None),
        P(None, "tensor"),
        P(None, None, "tensor"),
        P("tensor", None),
        P(None, "tensor"),
        P("tensor", None),
        P(),
        P(),
    )
    return jax.shard_map(local, mesh=mesh, in_specs=in_specs, out_specs=out_specs, check_vma=False)
```

profile of v0, /device:TPU:0, one launch (start us, length us, event | category | flops | bytes accessed | tf_op | source)
XLA Modules:
  0.0 1388.1 jit_solution(6832156781843160670)
XLA Ops:
  14.2 18.6 %while.174 = (s32[]{:T(128)}, bf16[2,512,192]{1,2,0:T(8,128)(2,1)}, f32[2,3,512]{2,1,0:T(4,128)S(1)}, s32[2]{0:T(128)}, s32[]{:T(128)}, /*index=5*/bf16[1024,192...) while((s32[]{:T(128)}, bf16[2,512,192]{1,2,0:T(8,128)(2,1)}, ...), condition=%wide.region_3.4_spmd, body=%wide.region_0.3_spmd.sunk | while | flops 422674432 | bytes 26145028 | solution.py:82
  44.2 56.1 %reduce-scatter.15.cloned.1.call-done = f32[256,768]{1,0:T(8,128)} async-done(((f32[1024,768]{1,0:T(8,128)}), f32[256,768]{1,0:T(8,128)}) %reduce-scatter.15.cloned.1.call-update) | async-done | bytes 786448 | tf_op jit(solution)/shard_map/while/body/eval_jaxpr/reduce_scatter | solution.py:173
  103.8 15.5 %while.176 = (s32[]{:T(128)}, bf16[2,512,192]{1,2,0:T(8,128)(2,1)S(1)}, f32[2,3,512]{2,1,0:T(4,128)S(1)}, s32[2]{0:T(128)S(1)}, s32[]{:T(128)}, /*index=5*/bf16[...) while((s32[]{:T(128)}, ...), condition=%wide.region_20.21_spmd, body=%wide.region_17.20_spmd.sunk | while | flops 422674432 | bytes 22999244 | solution.py:82
  123.7 2.4 fusion.178
  126.8 14.0 %all-gather.11.cloned.1.call-done = bf16[1024,768]{1,0:T(8,128)(2,1)} async-done(((bf16[256,768]{1,0:T(8,128)(2,1)}), bf16[1024,768]{1,0:T(8,128)(2,1)}) %all-gather.11.cloned.1.call-update) | async-done | bytes 1572880 | tf_op jit(solution)/shard_map/while/body/eval_jaxpr/all_gather | solution.py:177
  142.9 13.4 while.175
  157.2 2.3 fusion.318
  159.6 42.6 %reduce-scatter.21.cloned.1.call-done = f32[256,768]{1,0:T(8,128)} async-done(((f32[1024,768]{1,0:T(8,128)}), f32[256,768]{1,0:T(8,128)}) %reduce-scatter.21.cloned.1.call-update) | async-done | bytes 786448 | tf_op jit(solution)/shard_map/while/body/eval_jaxpr/reduce_scatter | solution.py:173
  203.9 60.8 %reduce-scatter.17.cloned.1.call-done = f32[256,768]{1,0:T(8,128)} async-done(((f32[1024,768]{1,0:T(8,128)}), f32[256,768]{1,0:T(8,128)}) %reduce-scatter.17.cloned.1.call-update) | async-done | bytes 786448 | tf_op jit(solution)/shard_map/while/body/eval_jaxpr/reduce_scatter | solution.py:182
  264.8 2.6 fusion.301
  267.4 3.0 fusion.193
  274.9 29.7 %all-gather.15.cloned.1.call-done = bf16[1024,768]{1,0:T(8,128)(2,1)} async-done(((bf16[256,768]{1,0:T(8,128)(2,1)}), bf16[1024,768]{1,0:T(8,128)(2,1)}) %all-gather.15.cloned.1.call-update) | async-done | bytes 1572880 | tf_op jit(solution)/shard_map/while/body/eval_jaxpr/all_gather | solution.py:177
  308.0 16.1 %while.177 = (s32[]{:T(128)}, bf16[2,512,192]{1,2,0:T(8,128)(2,1)}, f32[2,3,512]{2,1,0:T(4,128)S(1)}, s32[]{:T(128)}, s32[2]{0:T(128)}, /*index=5*/bf16[1024,192...) while((s32[]{:T(128)}, bf16[2,512,192]{1,2,0:T(8,128)(2,1)}, ...), condition=%wide.region_27.28_spmd, body=%wide.region_24.27_spmd.sunk | while | flops 421625344 | bytes 25618716 | solution.py:82
  325.9 3.3 fusion.321
  329.3 13.2 all-gather.13.cloned.1.call-done
  342.6 10.4 multiply_convert_fusion.5
  354.2 3.1 fusion.319
  357.4 46.7 %reduce-scatter.23.cloned.1.call-done = f32[256,768]{1,0:T(8,128)} async-done(((f32[1024,768]{1,0:T(8,128)}), f32[256,768]{1,0:T(8,128)}) %reduce-scatter.23.cloned.1.call-update) | async-done | bytes 786448 | tf_op jit(solution)/shard_map/while/body/eval_jaxpr/reduce_scatter | solution.py:182
  406.7 60.0 %reduce-scatter.19.cloned.1.call-done = f32[256,768]{1,0:T(8,128)} async-done(((f32[1024,768]{1,0:T(8,128)}), f32[256,768]{1,0:T(8,128)}) %reduce-scatter.19.cloned.1.call-update) | async-done | bytes 786448 | tf_op jit(solution)/shard_map/while/body/eval_jaxpr/reduce_scatter | solution.py:190
  466.7 3.3 fusion.298
  470.2 37.0 %all-gather.17.cloned.1.call-done = bf16[1024,768]{1,0:T(8,128)(2,1)} async-done(((bf16[256,768]{1,0:T(8,128)(2,1)}), bf16[1024,768]{1,0:T(8,128)(2,1)}) %all-gather.17.cloned.1.call-update) | async-done | bytes 1572880 | tf_op jit(solution)/shard_map/while/body/eval_jaxpr/all_gather | solution.py:186
  507.2 10.5 multiply_convert_fusion.4
  518.9 3.0 fusion.322
  525.8 55.4 %reduce-scatter.25.cloned.1.call-done = f32[256,768]{1,0:T(8,128)} async-done(((f32[1024,768]{1,0:T(8,128)}), f32[256,768]{1,0:T(8,128)}) %reduce-scatter.25.cloned.1.call-update) | async-done | bytes 786448 | tf_op jit(solution)/shard_map/while/body/eval_jaxpr/reduce_scatter | solution.py:190
  584.4 2.4 fusion.297
  592.0 33.9 %all-gather.19.cloned.1.call-done = bf16[1024,768]{1,0:T(8,128)(2,1)} async-done(((bf16[256,768]{1,0:T(8,128)(2,1)}), bf16[1024,768]{1,0:T(8,128)(2,1)}) %all-gather.19.cloned.1.call-update) | async-done | bytes 1572880 | tf_op jit(solution)/shard_map/while/body/eval_jaxpr/all_gather | solution.py:195
  625.9 5.6 add_convert_fusion.3
  632.7 2.6 convolution_convert_fusion.1
  635.6 28.3 %all-gather.25.cloned.1.call-done = bf16[1024,768]{1,0:T(8,128)(2,1)} async-done(((bf16[256,768]{1,0:T(8,128)(2,1)}), bf16[1024,768]{1,0:T(8,128)(2,1)}) %all-gather.25.cloned.1.call-update) | async-done | bytes 1572880 | tf_op jit(solution)/shard_map/while/body/eval_jaxpr/all_gather | solution.py:195
  663.9 5.6 add_convert_fusion.1
  670.7 2.6 convolution_convert_fusion
  673.3 27.6 %reduce-scatter.27.cloned.1.call-done = bf16[256,768]{1,0:T(8,128)(2,1)} async-done(((bf16[1024,768]{1,0:T(8,128)(2,1)}), bf16[256,768]{1,0:T(8,128)(2,1)}) %reduce-scatter.27.cloned.1.call-update) | async-done | bytes 393232 | tf_op jit(solution)/shard_map/while/body/eval_jaxpr/reduce_scatter | solution.py:200
  701.0 37.0 %reduce-scatter.33.cloned.1.call-done = bf16[256,768]{1,0:T(8,128)(2,1)} async-done(((bf16[1024,768]{1,0:T(8,128)(2,1)}), bf16[256,768]{1,0:T(8,128)(2,1)}) %reduce-scatter.33.cloned.1.call-update) | async-done | bytes 393232 | tf_op jit(solution)/shard_map/while/body/eval_jaxpr/reduce_scatter | solution.py:200
  738.0 3.1 multiply_reduce_fusion.6
  741.3 3.3 fusion.293
  749.2 33.4 %all-gather.27.cloned.1.call-done = bf16[1024,768]{1,0:T(8,128)(2,1)} async-done(((bf16[256,768]{1,0:T(8,128)(2,1)}), bf16[1024,768]{1,0:T(8,128)(2,1)}) %all-gather.27.cloned.1.call-update) | async-done | bytes 1572880 | tf_op jit(solution)/shard_map/while/body/eval_jaxpr/all_gather | solution.py:204
  785.9 27.7 %while.180 = (s32[]{:T(128)}, f32[1024,3,64]{0,2,1:T(8,128)S(1)}, f32[1024,3,64]{0,2,1:T(8,128)}, bf16[2,512,192]{1,2,0:T(8,128)(2,1)}, s32[2]{0:T(128)}, /*inde...) while((s32[]{:T(128)}, f32[1024,3,64]{0,2,1:T(8,128)S(1)}, ...), condition=%wide.region_56.57_spmd.clone, body=%wide.region_54.56_spmd.clone.sunk | while | flops 1031405056 | bytes 63158656 | solution.py:131
  815.4 3.3 fusion.324
  823.2 26.0 %while.178 = (s32[]{:T(128)}, f32[1024,3,64]{0,2,1:T(8,128)S(1)}, f32[1024,3,64]{0,2,1:T(8,128)}, bf16[2,512,192]{1,2,0:T(8,128)(2,1)S(1)}, s32[2]{0:T(128)}, /*...) while((s32[]{:T(128)}, f32[1024,3,64]{0,2,1:T(8,128)S(1)}, ...), condition=%wide.region_41.42_spmd.clone, body=%wide.region_39.41_spmd.clone.sunk | while | flops 1031405056 | bytes 60012872 | solution.py:131
  849.3 3.5 fusion.323
  852.9 28.9 %reduce-scatter.35.cloned.1.call-done = f32[256,768]{1,0:T(8,128)} async-done(((f32[1024,768]{1,0:T(8,128)}), f32[256,768]{1,0:T(8,128)}) %reduce-scatter.35.cloned.1.call-update) | async-done | bytes 786448 | tf_op jit(solution)/shard_map/while/body/eval_jaxpr/reduce_scatter | solution.py:216
  881.8 62.5 %reduce-scatter.29.cloned.1.call-done = f32[256,768]{1,0:T(8,128)} async-done(((f32[1024,768]{1,0:T(8,128)}), f32[256,768]{1,0:T(8,128)}) %reduce-scatter.29.cloned.1.call-update) | async-done | bytes 786448 | tf_op jit(solution)/shard_map/while/body/eval_jaxpr/reduce_scatter | solution.py:216
  944.4 3.5 multiply_reduce_fusion.7
  947.9 2.6 fusion.292
  959.0 3.6 fusion.328
  964.5 2.9 convolution_add_fusion.2
  967.5 2.9 convolution_add_fusion.3
  976.4 2.3 convolution_add_fusion.1
  979.7 2.8 fusion.326
  982.5 7.1 all-gather.29.cloned.1.call-done
  992.9 29.8 %while.181 = (s32[]{:T(128)}, f32[1024,3,64]{0,2,1:T(8,128)S(1)}, f32[1024,3,64]{0,2,1:T(8,128)}, bf16[2,512,192]{1,2,0:T(8,128)(2,1)}, s32[2]{0:T(128)}, /*inde...) while((s32[]{:T(128)}, f32[1024,3,64]{0,2,1:T(8,128)S(1)}, ...), condition=%wide.region_62.63_spmd.clone, body=%wide.region_60.62_spmd.clone.sunk | while | flops 1032454144 | bytes 65257860 | solution.py:131
  1000.7 2.5 multiply_reduce_fusion.25
  1015.5 2.5 multiply_reduce_fusion.25
  1032.1 30.0 %while.179 = (s32[]{:T(128)}, f32[1024,3,64]{0,2,1:T(8,128)S(1)}, f32[1024,3,64]{0,2,1:T(8,128)}, bf16[2,512,192]{1,2,0:T(8,128)(2,1)}, s32[2]{0:T(128)}, /*inde...) while((s32[]{:T(128)}, f32[1024,3,64]{0,2,1:T(8,128)S(1)}, ...), condition=%wide.region_47.48_spmd.clone, body=%wide.region_45.47_spmd.clone.sunk | while | flops 1032454144 | bytes 65257860 | solution.py:131
  1039.9 2.5 multiply_reduce_fusion.23
  1054.9 2.5 multiply_reduce_fusion.23
  1068.1 3.0 maximum_add_fusion.1
  1083.8 43.0 %all-reduce = (f32[3,768]{1,0:T(4,128)}, f32[3,768]{1,0:T(4,128)}) all-reduce(f32[3,768]{1,0:T(4,128)S(1)} %maximum_add_fusion.2, f32[3,768]{1,0:T(4,128)S(1)} %maximum_add_fusion.3), channel_id=1, replica_groups=mesh['dp'=8,'tensor'=4] {'dp','tensor'}, use_global_device_ids=true, to_apply=%region_79.80 | all-reduce | flops 4608 | bytes 36864 | tf_op jit(solution)/shard_map/psum | solution.py:286
  1126.8 25.1 %reduce-scatter.39.cloned.1.call-done = f32[256,768]{1,0:T(8,128)} async-done(((f32[1024,768]{1,0:T(8,128)}), f32[256,768]{1,0:T(8,128)}) %reduce-scatter.39.cloned.1.call-update) | async-done | bytes 786448 | tf_op jit(solution)/shard_map/while/body/eval_jaxpr/reduce_scatter | solution.py:217
  1151.8 2.6 pad_maximum_fusion.1
  1154.4 35.7 %reduce-scatter.37.cloned.1.call-done = bf16[256,768]{1,0:T(8,128)(2,1)} async-done(((bf16[1024,768]{1,0:T(8,128)(2,1)}), bf16[256,768]{1,0:T(8,128)(2,1)}) %reduce-scatter.37.cloned.1.call-update) | async-done | bytes 393232 | tf_op jit(solution)/shard_map/while/body/eval_jaxpr/reduce_scatter | solution.py:240
  1191.3 35.3 %reduce-scatter.31.cloned.1.call-done = bf16[256,768]{1,0:T(8,128)(2,1)} async-done(((bf16[1024,768]{1,0:T(8,128)(2,1)}), bf16[256,768]{1,0:T(8,128)(2,1)}) %reduce-scatter.31.cloned.1.call-update) | async-done | bytes 393232 | tf_op jit(solution)/shard_map/while/body/eval_jaxpr/reduce_scatter | solution.py:240
  1229.0 142.8 %all-reduce.4.cloned.1.call-done = (f32[3,768,192]{1,2,0:T(8,128)}, f32[192,768]{1,0:T(8,128)}, f32[768,192]{0,1:T(8,128)}, f32[2,768,192]{1,2,0:T(8,128)}, f32[...) async-done(((f32[3,768,192]{1,2,0:T(8,128)}, f32[192,768]{1,0:T(8,128)}, f32[768,192]{0,1:T(8,128)}, f32[2,768,192]{1,2,0:T(8,128)}, f32[192,768]{1,0:T(8,128)}, ...) | async-done | bytes 9437200 | tf_op jit(solution)/shard_map/psum | solution.py:143
  1371.8 2.9 copy.145
  (785 shorter events, 274.1 us)
Async XLA Ops:
  7.2 335.4 %copy-start = (bf16[768,768]{1,0:T(8,128)(2,1)S(1)}, bf16[768,768]{1,0:T(8,128)(2,1)}, u32[]{:S(2)}) copy-start(bf16[768,768]{1,0:T(8,128)(2,1)} %param.40) | copy-start | bytes 3538948
  7.2 93.0 %reduce-scatter.15.cloned.1.call-start = ((), (), s32[]{:S(2)}) async-start(), calls=%async_computation.14 | async-start | bytes 3932160 | tf_op jit(solution)/shard_map/while/body/eval_jaxpr/reduce_scatter | solution.py:173
  14.2 20.7 %copy-start.89 = (bf16[192,768]{1,0:T(8,128)(2,1)S(1)}, bf16[192,768]{1,0:T(8,128)(2,1)}, u32[]{:S(2)}) copy-start(bf16[192,768]{1,0:T(8,128)(2,1)} %param.36) | copy-start | bytes 884740
  37.2 103.6 %all-gather.11.cloned.1.call-start = ((), (), s32[]{:S(2)}) async-start(), calls=%async_computation.15 | async-start | bytes 1966080 | tf_op jit(solution)/shard_map/while/body/eval_jaxpr/all_gather | solution.py:177
  42.3 60.2 %copy-start.110 = (f32[768]{0:T(1024)S(1)}, f32[768]{0:T(1024)}, u32[]{:S(2)}) copy-start(f32[768]{0:T(1024)} %get-tuple-element.1020) | copy-start | bytes 9220
  42.3 60.2 %copy-start.114 = (f32[768]{0:T(1024)S(1)}, f32[768]{0:T(1024)}, u32[]{:S(2)}) copy-start(f32[768]{0:T(1024)} %get-tuple-element.776) | copy-start | bytes 9220
  101.6 163.1 %copy-start.123 = (f32[256]{0:T(256)}, f32[256]{0:T(256)S(1)}, u32[]{:S(2)}) copy-start(f32[256]{0:T(256)S(1)} %broadcast_multiply_fusion.5) | copy-start | bytes 3076
  101.9 162.8 %copy-start.131 = (f32[256]{0:T(256)}, f32[256]{0:T(256)S(1)}, u32[]{:S(2)}) copy-start(f32[256]{0:T(256)S(1)} %fusion.272) | copy-start | bytes 3076
  103.5 98.8 %reduce-scatter.21.cloned.1.call-start = ((), (), s32[]{:S(2)}) async-start(), calls=%async_computation.19 | async-start | bytes 3932160 | tf_op jit(solution)/shard_map/while/body/eval_jaxpr/reduce_scatter | solution.py:173
  123.0 141.7 %reduce-scatter.17.cloned.1.call-start = ((), (), s32[]{:S(2)}) async-start(), calls=%async_computation.16 | async-start | bytes 3932160 | tf_op jit(solution)/shard_map/while/body/eval_jaxpr/reduce_scatter | solution.py:182
  123.7 17.1 %copy-start.88 = (bf16[768,192]{0,1:T(8,128)(2,1)S(1)}, bf16[768,192]{0,1:T(8,128)(2,1)}, u32[]{:S(2)}) copy-start(bf16[768,192]{0,1:T(8,128)(2,1)} %param.37) | copy-start | bytes 884740
  142.9 14.3 %copy-start.85 = (bf16[192,768]{1,0:T(8,128)(2,1)S(1)}, bf16[192,768]{1,0:T(8,128)(2,1)}, u32[]{:S(2)}) copy-start(bf16[192,768]{1,0:T(8,128)(2,1)} %param.39) | copy-start | bytes 884740
  156.3 45.9 %copy-start.106 = (f32[2,3,512]{2,1,0:T(4,128)}, f32[2,3,512]{2,1,0:T(4,128)S(1)}, u32[]{:S(2)}) copy-start(f32[2,3,512]{2,1,0:T(4,128)S(1)} %get-tuple-element.1686) | copy-start | bytes 36868
  159.5 105.2 %copy-start.111 = (f32[768]{0:T(1024)S(1)}, f32[768]{0:T(1024)}, u32[]{:S(2)}) copy-start(f32[768]{0:T(1024)} %get-tuple-element.1020) | copy-start | bytes 9220
  159.5 105.2 %copy-start.115 = (f32[768]{0:T(1024)S(1)}, f32[768]{0:T(1024)}, u32[]{:S(2)}) copy-start(f32[768]{0:T(1024)} %get-tuple-element.776) | copy-start | bytes 9220
  159.6 145.0 %all-gather.15.cloned.1.call-start = ((), (), s32[]{:S(2)}) async-start(), calls=%async_computation.20 | async-start | bytes 1966080 | tf_op jit(solution)/shard_map/while/body/eval_jaxpr/all_gather | solution.py:177
  203.7 200.4 %copy-start.8 = (f32[256,768]{1,0:T(8,128)}, f32[256,768]{1,0:T(8,128)S(1)}, u32[]{:S(2)}) copy-start(f32[256,768]{1,0:T(8,128)S(1)} %get-tuple-element.968) | copy-start | bytes 2359300
  203.7 63.7 %copy-start.121 = (f32[256]{0:T(256)}, f32[256]{0:T(256)S(1)}, u32[]{:S(2)}) copy-start(f32[256]{0:T(256)S(1)} %broadcast_multiply_fusion.2) | copy-start | bytes 3076
  203.9 66.5 %copy-start.157 = (f32[256]{0:T(256)}, f32[256]{0:T(256)S(1)}, u32[]{:S(2)}) copy-start(f32[256]{0:T(256)S(1)} %multiply_reduce_fusion.14) | copy-start | bytes 3076
  203.9 66.5 %copy-start.129 = (f32[256]{0:T(256)}, f32[256]{0:T(256)S(1)}, u32[]{:S(2)}) copy-start(f32[256]{0:T(256)S(1)} %fusion.275) | copy-start | bytes 3076
  267.3 75.2 %all-gather.13.cloned.1.call-start = ((), (), s32[]{:S(2)}) async-start(), calls=%async_computation.17 | async-start | bytes 1966080 | tf_op jit(solution)/shard_map/while/body/eval_jaxpr/all_gather | solution.py:186
  274.4 129.6 %reduce-scatter.23.cloned.1.call-start = ((), (), s32[]{:S(2)}) async-start(), calls=%async_computation.21 | async-start | bytes 3932160 | tf_op jit(solution)/shard_map/while/body/eval_jaxpr/reduce_scatter | solution.py:182
  329.3 137.4 %reduce-scatter.19.cloned.1.call-start = ((), (), s32[]{:S(2)}) async-start(), calls=%async_computation.18 | async-start | bytes 3932160 | tf_op jit(solution)/shard_map/while/body/eval_jaxpr/reduce_scatter | solution.py:190
  357.3 149.9 %all-gather.17.cloned.1.call-start = ((), (), s32[]{:S(2)}) async-start(), calls=%async_computation.22 | async-start | bytes 1966080 | tf_op jit(solution)/shard_map/while/body/eval_jaxpr/all_gather | solution.py:186
  405.5 112.1 %copy-start.116 = (f32[256]{0:T(256)}, f32[256]{0:T(256)S(1)}, u32[]{:S(2)}) copy-start(f32[256]{0:T(256)S(1)} %broadcast_multiply_fusion.1) | copy-start | bytes 3076
  406.6 111.1 %copy-start.161 = (f32[256]{0:T(256)}, f32[256]{0:T(256)S(1)}, u32[]{:S(2)}) copy-start(f32[256]{0:T(256)S(1)} %multiply_reduce_fusion.13) | copy-start | bytes 3076
  406.6 111.0 %copy-start.125 = (f32[256]{0:T(256)}, f32[256]{0:T(256)S(1)}, u32[]{:S(2)}) copy-start(f32[256]{0:T(256)S(1)} %fusion.276) | copy-start | bytes 3076
  470.0 111.3 %reduce-scatter.25.cloned.1.call-start = ((), (), s32[]{:S(2)}) async-start(), calls=%async_computation.23 | async-start | bytes 3932160 | tf_op jit(solution)/shard_map/while/body/eval_jaxpr/reduce_scatter | solution.py:190
  521.9 59.3 %copy-start.11 = (f32[256,768]{1,0:T(8,128)S(1)}, f32[256,768]{1,0:T(8,128)}, u32[]{:S(2)}) copy-start(f32[256,768]{1,0:T(8,128)} %copy-done.10) | copy-start | bytes 2359300
  521.9 104.0 %all-gather.19.cloned.1.call-start = ((), (), s32[]{:S(2)}) async-start(), calls=%async_computation.24 | async-start | bytes 1966080 | tf_op jit(solution)/shard_map/while/body/eval_jaxpr/all_gather | solution.py:195
  588.7 75.3 %all-gather.25.cloned.1.call-start = ((), (), s32[]{:S(2)}) async-start(), calls=%async_computation.30 | async-start | bytes 1966080 | tf_op jit(solution)/shard_map/while/body/eval_jaxpr/all_gather | solution.py:195
  592.0 109.0 %reduce-scatter.27.cloned.1.call-start = ((), (), s32[]{:S(2)}) async-start(), calls=%async_computation.25 | async-start | bytes 1966080 | tf_op jit(solution)/shard_map/while/body/eval_jaxpr/reduce_scatter | solution.py:200
  635.3 102.7 %reduce-scatter.33.cloned.1.call-start = ((), (), s32[]{:S(2)}) async-start(), calls=%async_computation.31 | async-start | bytes 1966080 | tf_op jit(solution)/shard_map/while/body/eval_jaxpr/reduce_scatter | solution.py:200
  673.3 67.9 %copy-start.14 = (f32[256,768]{1,0:T(8,128)S(1)}, f32[256,768]{1,0:T(8,128)}, u32[]{:S(2)}) copy-start(f32[256,768]{1,0:T(8,128)} %get-tuple-element.952) | copy-start | bytes 2359300
  673.3 109.3 %all-gather.27.cloned.1.call-start = ((), (), s32[]{:S(2)}) async-start(), calls=%async_computation.32 | async-start | bytes 1966080 | tf_op jit(solution)/shard_map/while/body/eval_jaxpr/all_gather | solution.py:204
  701.0 40.2 %copy-start.59 = (bf16[256,768]{1,0:T(8,128)(2,1)S(1)}, bf16[256,768]{1,0:T(8,128)(2,1)}, u32[]{:S(2)}) copy-start(bf16[256,768]{1,0:T(8,128)(2,1)} %reduce-scatter.27.cloned.1.call-done) | copy-start | bytes 1179652
  744.6 38.0 %copy-start.86 = (bf16[192,768]{1,0:T(8,128)(2,1)S(1)}, bf16[192,768]{1,0:T(8,128)(2,1)}, u32[]{:S(2)}) copy-start(bf16[192,768]{1,0:T(8,128)(2,1)} %param.39) | copy-start | bytes 884740
  744.6 41.3 %copy-start.29 = (bf16[1024,3,64]{0,2,1:T(8,128)(2,1)S(1)}, bf16[1024,3,64]{0,2,1:T(8,128)(2,1)}, u32[]{:S(2)}) copy-start(bf16[1024,3,64]{0,2,1:T(8,128)(2,1)} %get-tuple-element.1947) | copy-start | bytes 1179652
  744.6 41.3 %copy-start.165 = (f32[256]{0:T(256)}, f32[256]{0:T(256)S(1)}, u32[]{:S(2)}) copy-start(f32[256]{0:T(256)S(1)} %negate_multiply_fusion.3) | copy-start | bytes 3076
  746.3 74.2 %all-gather.21.cloned.1.call-start = ((), (), s32[]{:S(2)}) async-start(), calls=%async_computation.26 | async-start | bytes 1966080 | tf_op jit(solution)/shard_map/while/body/eval_jaxpr/all_gather | solution.py:204
  747.1 38.8 %copy-start.167 = (f32[256]{0:T(256)}, f32[256]{0:T(256)S(1)}, u32[]{:S(2)}) copy-start(f32[256]{0:T(256)S(1)} %negate_multiply_fusion.6) | copy-start | bytes 3076
  749.1 132.7 %reduce-scatter.35.cloned.1.call-start = ((), (), s32[]{:S(2)}) async-start(), calls=%async_computation.33 | async-start | bytes 3932160 | tf_op jit(solution)/shard_map/while/body/eval_jaxpr/reduce_scatter | solution.py:216
  818.7 125.6 %reduce-scatter.29.cloned.1.call-start = ((), (), s32[]{:S(2)}) async-start(), calls=%async_computation.27 | async-start | bytes 3932160 | tf_op jit(solution)/shard_map/while/body/eval_jaxpr/reduce_scatter | solution.py:216
  849.2 95.1 %copy-start.9 = (f32[256,768]{1,0:T(8,128)S(1)}, f32[256,768]{1,0:T(8,128)}, u32[]{:S(2)}) copy-start(f32[256,768]{1,0:T(8,128)} %copy-done.8) | copy-start | bytes 2359300
  849.3 95.0 %copy-start.112 = (f32[768]{0:T(1024)S(1)}, f32[768]{0:T(1024)}, u32[]{:S(2)}) copy-start(f32[768]{0:T(1024)} %get-tuple-element.1020) | copy-start | bytes 9220
  849.3 95.0 %copy-start.122 = (f32[256]{0:T(256)S(1)}, f32[256]{0:T(256)}, u32[]{:S(2)}) copy-start(f32[256]{0:T(256)} %copy-done.121) | copy-start | bytes 3076
  849.3 95.0 %copy-start.124 = (f32[256]{0:T(256)S(1)}, f32[256]{0:T(256)}, u32[]{:S(2)}) copy-start(f32[256]{0:T(256)} %copy-done.123) | copy-start | bytes 3076
  849.3 95.0 %copy-start.130 = (f32[256]{0:T(256)S(1)}, f32[256]{0:T(256)}, u32[]{:S(2)}) copy-start(f32[256]{0:T(256)} %copy-done.129) | copy-start | bytes 3076
  849.3 95.0 %copy-start.132 = (f32[256]{0:T(256)S(1)}, f32[256]{0:T(256)}, u32[]{:S(2)}) copy-start(f32[256]{0:T(256)} %copy-done.131) | copy-start | bytes 3076
  849.3 95.0 %copy-start.166 = (f32[256]{0:T(256)S(1)}, f32[256]{0:T(256)}, u32[]{:S(2)}) copy-start(f32[256]{0:T(256)} %copy-done.165) | copy-start | bytes 3076
  849.3 95.0 %copy-start.168 = (f32[256]{0:T(256)S(1)}, f32[256]{0:T(256)}, u32[]{:S(2)}) copy-start(f32[256]{0:T(256)} %copy-done.167) | copy-start | bytes 3076
  852.8 95.0 %copy-start.158 = (f32[256]{0:T(256)S(1)}, f32[256]{0:T(256)}, u32[]{:S(2)}) copy-start(f32[256]{0:T(256)} %copy-done.157) | copy-start | bytes 3076
  852.8 95.0 %copy-start.156 = (f32[256]{0:T(256)S(1)}, f32[256]{0:T(256)}, u32[]{:S(2)}) copy-start(f32[256]{0:T(256)} %copy-done.155) | copy-start | bytes 3076
  852.8 136.7 %all-gather.29.cloned.1.call-start = ((), (), s32[]{:S(2)}) async-start(), calls=%async_computation.34 | async-start | bytes 1966080 | tf_op jit(solution)/shard_map/while/body/eval_jaxpr/all_gather | solution.py:225
  952.3 76.4 %all-gather.23.cloned.1.call-start = ((), (), s32[]{:S(2)}) async-start(), calls=%async_computation.28 | async-start | bytes 1966080 | tf_op jit(solution)/shard_map/while/body/eval_jaxpr/all_gather | solution.py:225
  954.3 172.4 %reduce-scatter.41.cloned.1.call-start = ((), (), s32[]{:S(2)}) async-start(), calls=%async_computation.37 | async-start | bytes 3932160 | tf_op jit(solution)/shard_map/while/body/eval_jaxpr/reduce_scatter | solution.py:217
  958.7 193.1 %reduce-scatter.39.cloned.1.call-start = ((), (), s32[]{:S(2)}) async-start(), calls=%async_computation.36 | async-start | bytes 3932160 | tf_op jit(solution)/shard_map/while/body/eval_jaxpr/reduce_scatter | solution.py:217
  978.8 211.4 %reduce-scatter.37.cloned.1.call-start = ((), (), s32[]{:S(2)}) async-start(), calls=%async_computation.35 | async-start | bytes 1966080 | tf_op jit(solution)/shard_map/while/body/eval_jaxpr/reduce_scatter | solution.py:240
  1028.4 198.2 %reduce-scatter.31.cloned.1.call-start = ((), (), s32[]{:S(2)}) async-start(), calls=%async_computation.29 | async-start | bytes 1966080 | tf_op jit(solution)/shard_map/while/body/eval_jaxpr/reduce_scatter | solution.py:240
  1067.7 304.0 %all-reduce.4.cloned.1.call-start = ((), (), s32[]{:S(2)}) async-start(), calls=%async_computation.38 | async-start | bytes 18874368 | tf_op jit(solution)/shard_map/psum | solution.py:143
  1082.4 107.8 %copy-start.34 = (f32[256,768]{1,0:T(8,128)S(1)}, f32[256,768]{1,0:T(8,128)}, u32[]{:S(2)}) copy-start(f32[256,768]{1,0:T(8,128)} %copy-done.33) | copy-start | bytes 2359300
  1082.4 107.8 %copy-start.151 = (f32[256]{0:T(256)S(1)}, f32[256]{0:T(256)}, u32[]{:S(2)}) copy-start(f32[256]{0:T(256)} %copy-done.150) | copy-start | bytes 3076
  1082.6 144.0 %copy-start.32 = (f32[256,768]{1,0:T(8,128)S(1)}, f32[256,768]{1,0:T(8,128)}, u32[]{:S(2)}) copy-start(f32[256,768]{1,0:T(8,128)} %get-tuple-element.940) | copy-start | bytes 2359300
  1082.6 144.0 %copy-start.153 = (f32[256]{0:T(256)S(1)}, f32[256]{0:T(256)}, u32[]{:S(2)}) copy-start(f32[256]{0:T(256)} %copy-done.152) | copy-start | bytes 3076
  (166 other events, 456.9 us)
Sparse Core Ops, SparseCore 0:
  37.3 62.9 reduce-scatter.14
  103.6 37.1 all-gather.10
  143.1 59.1 reduce-scatter.20
  204.4 60.2 reduce-scatter.16
  267.5 37.0 all-gather.14
  306.6 35.9 all-gather.12
  344.9 59.1 reduce-scatter.22
  406.4 60.2 reduce-scatter.18
  470.1 37.0 all-gather.16
  522.0 59.1 reduce-scatter.24
  588.8 37.1 all-gather.18
  627.9 35.9 all-gather.24
  666.8 34.1 reduce-scatter.26
  703.7 34.2 reduce-scatter.32
  746.4 36.0 all-gather.26
  784.5 35.9 all-gather.20
  822.7 59.0 reduce-scatter.34
  884.0 60.2 reduce-scatter.28
  952.4 37.1 all-gather.28
  990.9 35.9 all-gather.22
  1029.3 59.0 reduce-scatter.40
  1090.7 61.0 reduce-scatter.38
  1154.7 35.4 reduce-scatter.36
  1192.3 34.2 reduce-scatter.30
  1232.5 139.2 all-reduce.3
where the time goes:
time: 1400 us; the launch traced here: 1390 us
  waiting for transfers between devices  915 us (65%)
  matrix products  210 us (15%)
  other arithmetic  100 us (7%)
  local copies, waits for them, and re-layouts  73.9 us (5%)
  blocking collectives  43 us (3%)
  loops' own time  26 us (2%)
  between operations  16.8 us (1%)
    psum x1, waiting for transfers between devices, reduce_weights(): lax.psum((grads[0], grads[1], grads[2], grads[3], grads[4], grads[5], gra...  143 us
    reduce_scatter x2, waiting for transfers between devices, sequence(): lax.psum_scatter(dot_nn(hidden_low, ffn_out), 'tensor', scatter_dimension...  115 us
    reduce_scatter x2, waiting for transfers between devices, sequence(): lax.psum_scatter(dot_nn(attn_cross, cross_out), 'tensor', scatter_dimensi...  107 us
    reduce_scatter x2, waiting for transfers between devices, sequence(): lax.psum_scatter(dot_nn(attn_self, self_out), 'tensor', scatter_dimension...  98.7 us
    reduce_scatter x2, waiting for transfers between devices, sequence(): lax.psum_scatter(dot_nt(grad_qc, cross_q), 'tensor', scatter_dimension=0,...  91.4 us
    reduce_scatter x2, waiting for transfers between devices, sequence(): lax.psum_scatter((part_q + part_k + part_v).astype(jnp.bfloat16), 'tensor...  71 us
    reduce_scatter x2, waiting for transfers between devices, sequence(): lax.psum_scatter(dot_nt(grad_pre, ffn_in).astype(jnp.bfloat16), 'tensor',...  64.6 us
    all_gather x2, waiting for transfers between devices, sequence(): lax.all_gather(grad_res3.astype(jnp.bfloat16), 'tensor', axis=0, tiled=True)  62.2 us
  transfers between devices with their start and end apart: 25, of which 23 were waited for; matrix products, arithmetic and copies ran while one was open for 20% of the time, Pallas kernels for 0%

commit v1 on v0

v1 whole, which is shorter than its diff:
```python
import functools

import jax
import jax.numpy as jnp
from jax import lax
from jax.experimental import pallas as pl
from jax.experimental.pallas import tpu as pltpu
from jax.sharding import PartitionSpec as P

HEAD = 64
EPS = 1e-05
NEG = -1e30
LOW = jnp.bfloat16
F32 = jnp.float32
OWN_BLOCKS = ((0, 3), (1, 2))
MIB = 1024 * 1024


def dot_nn(left, right):
    return lax.dot_general(left, right, (((1,), (0,)), ((), ())), preferred_element_type=F32)


def dot_nt(left, right):
    return lax.dot_general(left, right, (((1,), (1,)), ((), ())), preferred_element_type=F32)


def dot_tn(left, right):
    return lax.dot_general(left, right, (((0,), (0,)), ((), ())), preferred_element_type=F32)


def cost(flops, size, trans=0):
    return pl.CostEstimate(flops=int(flops), bytes_accessed=int(size), transcendentals=int(trans))


def whole(shape):
    return pl.BlockSpec(shape, lambda *_: (0,) * len(shape), pipeline_mode=pl.Buffered(1))


def attend_forward(causal, info, query, keys_in, values_in):
    rows, width = query.shape
    key_rows = keys_in.shape[0]
    block = rows // 2
    pair = 2 * HEAD

    def kernel(info_ref, q_ref, k_ref, v_ref, o_ref, lse_ref):
        length = info_ref[1]

        def part(spot, block_id, extent):
            lane = lax.broadcasted_iota(jnp.int32, (block, pair), 1)
            limit = jnp.full((block, 1), length, jnp.int32)
            if causal:
                row = block_id * block + lax.broadcasted_iota(jnp.int32, (block, 1), 0)
                limit = jnp.minimum(limit, row + 1)
            allowed = lax.broadcasted_iota(jnp.int32, (block, extent), 1) < limit
            span = pl.ds(spot * block, block)
            q = q_ref[span, :]
            out, logs = None, None
            for side in range(2):
                mine = (lane >= HEAD) if side else (lane < HEAD)
                q_side = jnp.where(mine, q, 0).astype(LOW) * LOW(HEAD ** (-0.5))
                scores = jnp.where(allowed, dot_nt(q_side, k_ref[:extent, :]), NEG)
                peak = jnp.max(scores, -1, keepdims=True)
                weights = jnp.exp(scores - peak)
                total = jnp.sum(weights, -1, keepdims=True)
                mixed = dot_nn(weights.astype(LOW), v_ref[:extent, :]) / total
                log_total = peak + jnp.log(total)
                if side:
                    out = jnp.where(mine, mixed, out)
                    logs = jnp.where(mine, log_total, logs)
                else:
                    out, logs = mixed, jnp.broadcast_to(log_total, (block, pair))
            o_ref[span, :] = out.astype(LOW)
            lse_ref[span, :] = logs

        if causal:
            for variant in range(2):

                @pl.when(info_ref[0] == variant)
                def _():
                    for spot in range(2):
                        block_id = OWN_BLOCKS[variant][spot]
                        part(spot, block_id, (block_id + 1) * block)
        else:
            for spot in range(2):
                part(spot, 0, key_rows)

    column = pl.BlockSpec((rows, pair), lambda p, *_: (0, p))
    key_column = pl.BlockSpec((key_rows, pair), lambda p, *_: (0, p))
    share = 0.625 if causal else 1.0
    elements = width // HEAD * rows * key_rows * share
    return pl.pallas_call(
        kernel,
        out_shape=(
            jax.ShapeDtypeStruct((rows, width), LOW),
            jax.ShapeDtypeStruct((rows, width), F32),
        ),
        grid_spec=pltpu.PrefetchScalarGridSpec(
            num_scalar_prefetch=1,
            grid=(width // pair,),
            in_specs=[column, key_column, key_column],
            out_specs=[column, column],
        ),
        compiler_params=pltpu.CompilerParams(vmem_limit_bytes=48 * MIB),
        cost_estimate=cost(elements * 1024, 10 * MIB, elements),
    )(info, query, keys_in, values_in)


def attend_backward(causal, info, query, keys_in, values_in, out, logs, grad_out):
    rows, width = query.shape
    key_rows = keys_in.shape[0]
    block = rows // 2
    pair = 2 * HEAD

    def kernel(
        info_ref, q_ref, k_ref, v_ref, o_ref, lse_ref, g_ref,
        dq_ref, dk_ref, dv_ref, dks_ref, dvs_ref, dk_acc, dv_acc,
    ):
        length = info_ref[1]
        dk_acc[...] = jnp.zeros_like(dk_acc)
        dv_acc[...] = jnp.zeros_like(dv_acc)

        def part(spot, block_id, extent):
            lane = lax.broadcasted_iota(jnp.int32, (block, pair), 1)
            limit = jnp.full((block, 1), length, jnp.int32)
            if causal:
                row = block_id * block + lax.broadcasted_iota(jnp.int32, (block, 1), 0)
                limit = jnp.minimum(limit, row + 1)
            allowed = lax.broadcasted_iota(jnp.int32, (block, extent), 1) < limit
            span = pl.ds(spot * block, block)
            q = q_ref[span, :]
            g = g_ref[span, :]
            along = g.astype(F32) * o_ref[span, :].astype(F32)
            dq = None
            for side in range(2):
                mine = (lane >= HEAD) if side else (lane < HEAD)
                q_side = jnp.where(mine, q, 0).astype(LOW) * LOW(HEAD ** (-0.5))
                g_side = jnp.where(mine, g, 0).astype(LOW)
                inner = jnp.sum(jnp.where(mine, along, 0.0), -1, keepdims=True)
                log_total = lse_ref[span, side * HEAD : side * HEAD + 1]
                scores = jnp.where(allowed, dot_nt(q_side, k_ref[:extent, :]), NEG)
                weights = jnp.exp(scores - log_total)
                dv_acc[:extent, :] += dot_tn(weights.astype(LOW), g_side)
                grad_w = dot_nt(g_side, v_ref[:extent, :])
                grad_s = (weights * (grad_w - inner)).astype(LOW)
                dk_acc[:extent, :] += dot_tn(grad_s, q_side)
                part_q = dot_nn(grad_s, k_ref[:extent, :])
                dq = jnp.where(mine, part_q, dq) if side else part_q
            dq_ref[span, :] = (dq * HEAD ** (-0.5)).astype(LOW)

        for variant in range(2):

            @pl.when(info_ref[0] == variant)
            def _():
                for spot in range(2):
                    block_id = OWN_BLOCKS[variant][spot]
                    part(spot, block_id, (block_id + 1) * block if causal else key_rows)
                for spot in range(2):
                    keep = slice(OWN_BLOCKS[variant][spot] * block, (OWN_BLOCKS[variant][spot] + 1) * block)
                    give = slice(OWN_BLOCKS[1 - variant][spot] * block, (OWN_BLOCKS[1 - variant][spot] + 1) * block)
                    span = slice(spot * block, (spot + 1) * block)
                    dk_ref[span, :] = dk_acc[keep, :].astype(LOW)
                    dv_ref[span, :] = dv_acc[keep, :].astype(LOW)
                    dks_ref[span, :] = dk_acc[give, :].astype(LOW)
                    dvs_ref[span, :] = dv_acc[give, :].astype(LOW)

    column = pl.BlockSpec((rows, pair), lambda p, *_: (0, p))
    key_column = pl.BlockSpec((key_rows, pair), lambda p, *_: (0, p))
    share = 0.625 if causal else 1.0
    elements = width // HEAD * rows * key_rows * share
    return pl.pallas_call(
        kernel,
        out_shape=(jax.ShapeDtypeStruct((rows, width), LOW),) * 5,
        grid_spec=pltpu.PrefetchScalarGridSpec(
            num_scalar_prefetch=1,
            grid=(width // pair,),
            in_specs=[column, key_column, key_column, column, column, column],
            out_specs=[column] * 5,
            scratch_shapes=[pltpu.VMEM((key_rows, pair), F32), pltpu.VMEM((key_rows, pair), F32)],
        ),
        compiler_params=pltpu.CompilerParams(vmem_limit_bytes=48 * MIB),
        cost_estimate=cost(elements * 2560, 10 * MIB, elements),
    )(info, query, keys_in, values_in, out, logs, grad_out)


def normalize(resid):
    center = resid - jnp.mean(resid, -1, keepdims=True)
    rstd = lax.rsqrt(jnp.mean(center * center, -1, keepdims=True) + EPS)
    return center * rstd, rstd


def norm_back(grad, gain, normed, rstd):
    dn = grad * gain
    mean_dn = jnp.mean(dn, -1, keepdims=True)
    mean_dnn = jnp.mean(dn * normed, -1, keepdims=True)
    return rstd * (dn - mean_dn - normed * mean_dnn)


def row_sum(value):
    return jnp.sum(value, 0, keepdims=True)


def first_norm(attn, x_rows, w_out, w_query, gain, shift):
    rows, width = attn.shape
    block = min(256, rows)

    def kernel(o_ref, x_ref, wo_ref, wq_ref, g_ref, s_ref, n_ref, r_ref, h_ref, q_ref):
        normed, rstd = normalize(x_ref[...].astype(F32) + dot_nn(o_ref[...], wo_ref[...]))
        n_ref[...] = normed
        r_ref[...] = jnp.broadcast_to(rstd, r_ref.shape)
        low = (normed * g_ref[0:1, :] + s_ref[0:1, :]).astype(LOW)
        h_ref[...] = low
        q_ref[...] = dot_nt(low, wq_ref[...]).astype(LOW)

    row = pl.BlockSpec((block, width), lambda b: (b, 0))
    thin = pl.BlockSpec((block, 128), lambda b: (b, 0))
    return pl.pallas_call(
        kernel,
        grid=(rows // block,),
        out_shape=(
            jax.ShapeDtypeStruct((rows, width), F32),
            jax.ShapeDtypeStruct((rows, 128), F32),
            jax.ShapeDtypeStruct((rows, width), LOW),
            jax.ShapeDtypeStruct((rows, width), LOW),
        ),
        in_specs=[row, row, whole(w_out.shape), whole(w_query.shape), whole(gain.shape), whole(shift.shape)],
        out_specs=[row, thin, row, row],
        compiler_params=pltpu.CompilerParams(vmem_limit_bytes=40 * MIB),
        cost_estimate=cost(4 * rows * width * width, 8 * MIB),
    )(attn, x_rows, w_out, w_query, gain, shift)


def gelu_parts(u):
    t = 1.0 / (1.0 + (0.3275911 * 0.7071067811865476) * jnp.abs(u))
    bell = jnp.exp(-0.5 * u * u)
    poly = t * (0.254829592 + t * (-0.284496736 + t * (1.421413741 + t * (-1.453152027 + t * 1.061405429))))
    tail = 0.5 * poly * bell
    return jnp.where(u < 0, tail, 1.0 - tail), bell * 0.3989422804014327


def middle(normed_one, attn, grad_y, w_out, w_up, w_down, gain, shift):
    rows, width = attn.shape
    hidden = w_up.shape[0]
    block = min(128, rows)
    step = min(768, hidden)

    def kernel(
        n0_ref, o_ref, y_ref, wo_ref, up_ref, dn_ref, g_ref, s_ref,
        out_ref, a_ref, du_ref, db3_ref, h2_ref, db2_ref, do_ref, dr2_ref, sums_ref, slope_ref,
    ):
        @pl.when(pl.program_id(0) == 0)
        def _():
            sums_ref[...] = jnp.zeros_like(sums_ref)

        h1 = n0_ref[...] * g_ref[0:1, :] + s_ref[0:1, :]
        n1, rstd1 = normalize(h1 + dot_nn(o_ref[...], wo_ref[...]))
        h2 = n1 * g_ref[1:2, :] + s_ref[1:2, :]
        h2_low = h2.astype(LOW)
        h2_ref[...] = h2_low
        branch = None
        for start in range(0, hidden, step):
            span = slice(start, start + step)
            u = dot_nt(h2_low, up_ref[span, :])
            share, density = gelu_parts(u)
            slope_ref[:, span] = share + u * density
            a = (u * share).astype(LOW)
            a_ref[:, span] = a
            term = dot_nn(a, dn_ref[span, :])
            branch = term if branch is None else branch + term
        n2, rstd2 = normalize(h2 + branch)
        out_ref[...] = (n2 * g_ref[2:3, :] + s_ref[2:3, :]).astype(LOW)
        g = y_ref[...].astype(F32)
        sums_ref[2:3, :] += row_sum(g * n2)
        sums_ref[5:6, :] += row_sum(g)
        dr3 = norm_back(g, g_ref[2:3, :], n2, rstd2)
        db3 = dr3.astype(LOW)
        db3_ref[...] = db3
        dh2 = dr3
        for start in range(0, hidden, step):
            span = slice(start, start + step)
            du = (dot_nt(db3, dn_ref[span, :]) * slope_ref[:, span]).astype(LOW)
            du_ref[:, span] = du
            dh2 = dh2 + dot_nn(du, up_ref[span, :])
        sums_ref[1:2, :] += row_sum(dh2 * n1)
        sums_ref[4:5, :] += row_sum(dh2)
        dr2 = norm_back(dh2, g_ref[1:2, :], n1, rstd1)
        dr2_ref[...] = dr2
        db2 = dr2.astype(LOW)
        db2_ref[...] = db2
        do_ref[...] = dot_nt(db2, wo_ref[...]).astype(LOW)

    row = pl.BlockSpec((block, width), lambda b: (b, 0))
    broad = pl.BlockSpec((block, hidden), lambda b: (b, 0))
    low_row = jax.ShapeDtypeStruct((rows, width), LOW)
    low_broad = jax.ShapeDtypeStruct((rows, hidden), LOW)
    return pl.pallas_call(
        kernel,
        grid=(rows // block,),
        out_shape=(
            low_row, low_broad, low_broad, low_row, low_row, low_row, low_row,
            jax.ShapeDtypeStruct((rows, width), F32),
            jax.ShapeDtypeStruct((8, width), F32),
        ),
        in_specs=[
            row, row, row, whole(w_out.shape), whole(w_up.shape), whole(w_down.shape),
            whole(gain.shape), whole(shift.shape),
        ],
        out_specs=[
            row, broad, broad, row, row, row, row, row,
            pl.BlockSpec((8, width), lambda b: (0, 0)),
        ],
        scratch_shapes=[pltpu.VMEM((block, hidden), F32)],
        compiler_params=pltpu.CompilerParams(vmem_limit_bytes=50 * MIB),
        cost_estimate=cost(rows * width * (8 * hidden + 4 * width), 24 * MIB, rows * hidden),
    )(normed_one, attn, grad_y, w_out, w_up, w_down, gain, shift)


def first_norm_back(grad_resid, grad_query, normed_one, rstd_one, w_query, w_out, gain):
    rows, width = grad_resid.shape
    block = min(256, rows)

    def kernel(dr2_ref, dq_ref, n_ref, r_ref, wq_ref, wo_ref, g_ref, dr1_ref, db1_ref, do_ref, sums_ref):
        @pl.when(pl.program_id(0) == 0)
        def _():
            sums_ref[...] = jnp.zeros_like(sums_ref)

        normed = n_ref[...]
        dh1 = dr2_ref[...] + dot_nn(dq_ref[...], wq_ref[...])
        sums_ref[0:1, :] += row_sum(dh1 * normed)
        sums_ref[3:4, :] += row_sum(dh1)
        dr1 = norm_back(dh1, g_ref[0:1, :], normed, r_ref[:, 0:1])
        dr1_ref[...] = dr1
        db1 = dr1.astype(LOW)
        db1_ref[...] = db1
        do_ref[...] = dot_nt(db1, wo_ref[...]).astype(LOW)

    row = pl.BlockSpec((block, width), lambda b: (b, 0))
    thin = pl.BlockSpec((block, 128), lambda b: (b, 0))
    low_row = jax.ShapeDtypeStruct((rows, width), LOW)
    return pl.pallas_call(
        kernel,
        grid=(rows // block,),
        out_shape=(
            jax.ShapeDtypeStruct((rows, width), F32), low_row, low_row,
            jax.ShapeDtypeStruct((8, width), F32),
        ),
        in_specs=[row, row, row, thin, whole(w_query.shape), whole(w_out.shape), whole(gain.shape)],
        out_specs=[row, row, row, pl.BlockSpec((8, width), lambda b: (0, 0))],
        compiler_params=pltpu.CompilerParams(vmem_limit_bytes=40 * MIB),
        cost_estimate=cost(4 * rows * width * width, 8 * MIB),
    )(grad_resid, grad_query, normed_one, rstd_one, w_query, w_out, gain)


def swap(value, axis, bit, size):
    return lax.ppermute(value, axis, [(d, d ^ bit) for d in range(size)])


def ordered(own, other, bit, axis):
    low = jnp.where(bit, other, own)
    high = jnp.where(bit, own, other)
    return jnp.concatenate([low, high], axis)


class Place:
    def __init__(self):
        self.dp = lax.axis_size("dp")
        self.tensor = lax.axis_size("tensor")
        index = lax.axis_index("dp")
        self.z = lax.axis_index("tensor")
        self.core = index & 1
        self.bits = {2: (index >> 1) & 1, 4: (index >> 2) & 1}


def gather_weights(place, shard, order):
    count, rows, width = shard.shape
    half, quarter = width // 2, rows // 4
    first, second = order
    at_row = (2 * place.bits[first] + place.bits[second]) * quarter
    piece = lax.dynamic_slice(
        shard, (0, at_row, place.core * half), (count, quarter, half)
    )
    got = jnp.stack([swap(piece, "tensor", r, place.tensor) for r in range(1, place.tensor)], 1)
    got = ordered(got, swap(got, "dp", second, place.dp), place.bits[second] == 1, 2)
    got = ordered(got, swap(got, "dp", first, place.dp), place.bits[first] == 1, 2)
    got = ordered(got, swap(got, "dp", 1, place.dp), place.core == 1, 3)
    return jnp.concatenate([shard[:, None], got], 1)


def reduce_grads(place, pairs, order):
    width = pairs[0][1].shape[1]
    half = width // 2
    slots = place.tensor
    rows = pairs[0][0].shape[1] // slots
    first, second = order

    def product(at):
        return jnp.stack(
            [dot_tn(g, lax.dynamic_slice_in_dim(a, at, half, 1)) for g, a in pairs]
        ).reshape(len(pairs), slots, rows, half)

    give = product((1 - place.core) * half).astype(LOW)
    total = product(place.core * half) + swap(give, "dp", 1, place.dp).astype(F32)
    for bit in order:
        rows = rows // 2
        mine = place.bits[bit]
        give = lax.dynamic_slice_in_dim(total, (1 - mine) * rows, rows, 2).astype(LOW)
        keep = lax.dynamic_slice_in_dim(total, mine * rows, rows, 2)
        total = keep + swap(give, "dp", bit, place.dp).astype(F32)
    low = total.astype(LOW)
    piece = total[:, 0]
    for r in range(1, slots):
        piece = piece + swap(low[:, r], "tensor", r, slots).astype(F32)
    bit = 8
    while bit < place.dp:
        piece = piece + swap(piece.astype(LOW), "dp", bit, place.dp).astype(F32)
        bit *= 2
    piece = piece.astype(LOW)
    piece = ordered(piece, swap(piece, "dp", second, place.dp), place.bits[second] == 1, 1)
    piece = ordered(piece, swap(piece, "dp", first, place.dp), place.bits[first] == 1, 1)
    piece = ordered(piece, swap(piece, "dp", 1, place.dp), place.core == 1, 2)
    return piece.astype(F32)


def local(
    inputs, memory, cotangent, dec_len, mem_len,
    self_qkv, self_out, cross_q, cross_kv, cross_out, ffn_in, ffn_out, ln_gain, ln_bias,
):
    place = Place()
    dp, slots = place.dp, place.tensor
    both = ("dp", "tensor")
    width = inputs.shape[3]
    length = inputs.shape[2]
    block = length // slots
    micro = place.z // 2
    owner = place.core == (place.z & 1)
    fetch_perm = [
        (d * slots + t, (d ^ 1) * slots + t)
        for d in range(dp)
        for t in range(slots)
        if d % 2 == t % 2
    ]
    spread = []
    for call in range(2):
        spread.append(
            [
                ((g + hh) * slots + s, (g + s % 2) * slots + OWN_BLOCKS[hh][(call + s // 2) % 2])
                for g in range(0, dp, 2)
                for s in range(slots)
                for hh in range(2)
            ]
        )
    collect = [[(dst, src) for src, dst in perm] for perm in spread]

    def fetch(value):
        mine = lax.dynamic_index_in_dim(value, micro, 0, False)[0]
        return jnp.where(owner, mine, lax.ppermute(mine, both, fetch_perm))

    def own_rows(value):
        return jnp.concatenate(
            [
                lax.dynamic_slice_in_dim(value, place.core * block, block, 0),
                lax.dynamic_slice_in_dim(value, (3 - place.core) * block, block, 0),
            ],
            0,
        )

    def send_rows(value):
        got = [
            lax.ppermute(
                lax.dynamic_slice_in_dim(value, ((call + micro) % 2) * block, block, 0), both, spread[call]
            )
            for call in range(2)
        ]
        near = place.z // 2 == 0
        return jnp.stack([jnp.where(near, got[0], got[1]), jnp.where(near, got[1], got[0])])[:, None]

    def collect_rows(value):
        got = [
            lax.ppermute(
                lax.dynamic_index_in_dim(value, (place.z // 2 + call) % 2, 0, False)[0], both, collect[call]
            )
            for call in range(2)
        ]
        return jnp.concatenate(
            [jnp.where(micro == 0, got[0], got[1]), jnp.where(micro == 0, got[1], got[0])], 0
        )

    def flat(weights):
        return weights.reshape(-1, width)

    lens = fetch(jnp.stack([dec_len, mem_len], -1))
    core = place.core.astype(jnp.int32)
    info_self = jnp.stack([core, lens[0]])
    info_cross = jnp.stack([core, lens[1]])

    x_all = fetch(inputs)
    w_qkv = gather_weights(place, jnp.swapaxes(self_qkv, 1, 2), (2, 4))
    w_mid = gather_weights(
        place,
        jnp.concatenate(
            [self_out[None], cross_q.T[None], jnp.swapaxes(cross_kv, 1, 2), cross_out[None]], 0
        ),
        (4, 2),
    )
    mem_all = fetch(memory)
    w_up = flat(gather_weights(place, ffn_in.T[None], (2, 4)))
    w_down = flat(gather_weights(place, ffn_out[None], (4, 2)))
    grad_y = collect_rows(cotangent)

    x_own = own_rows(x_all)
    mem_own = own_rows(mem_all)
    wq, wk, wv = (flat(w_qkv[t]) for t in range(3))
    w_so, w_cq, w_ck, w_cv, w_co = (flat(w_mid[t]) for t in range(5))

    query_s = dot_nt(x_own, wq).astype(LOW)
    key_s = dot_nt(x_all, wk).astype(LOW)
    value_s = dot_nt(x_all, wv).astype(LOW)
    attn_s, logs_s = attend_forward(True, info_self, query_s, key_s, value_s)
    normed_one, rstd_one, h1_low, query_c = first_norm(attn_s, x_own, w_so, w_cq, ln_gain, ln_bias)
    key_c = dot_nt(mem_all, w_ck).astype(LOW)
    value_c = dot_nt(mem_all, w_cv).astype(LOW)
    attn_c, logs_c = attend_forward(False, info_cross, query_c, key_c, value_c)
    (out_rows, act, grad_pre, grad_b3, h2_low, grad_b2, grad_oc, grad_r2, sums_late) = middle(
        normed_one, attn_c, grad_y, w_co, w_up, w_down, ln_gain, ln_bias
    )
    out = send_rows(out_rows)
    d_down = reduce_grads(place, [(act, grad_b3)], (2, 4))
    d_up = reduce_grads(place, [(grad_pre, h2_low)], (4, 2))

    dq_c, dk_c, dv_c, dk_cs, dv_cs = attend_backward(
        False, info_cross, query_c, key_c, value_c, attn_c, logs_c, grad_oc
    )
    dk_c = (dk_c.astype(F32) + swap(dk_cs, "dp", 1, dp).astype(F32)).astype(LOW)
    dv_c = (dv_c.astype(F32) + swap(dv_cs, "dp", 1, dp).astype(F32)).astype(LOW)
    grad_r1, grad_b1, grad_os, sums_first = first_norm_back(
        grad_r2, dq_c, normed_one, rstd_one, w_cq, w_so, ln_gain
    )
    d_mem = send_rows((dot_nn(dk_c, w_ck) + dot_nn(dv_c, w_cv)).astype(LOW)).astype(F32)
    d_mid = reduce_grads(
        place,
        [(attn_s, grad_b1), (dq_c, h1_low), (dk_c, mem_own), (dv_c, mem_own), (attn_c, grad_b2)],
        (2, 4),
    )

    sums = sums_late + sums_first
    bit = 1
    while bit < dp:
        sums = sums + swap(sums, "dp", bit, dp)
        bit *= 2
    bit = 1
    while bit < slots:
        sums = sums + swap(sums, "tensor", bit, slots)
        bit *= 2

    dq_s, dk_s, dv_s, dk_ss, dv_ss = attend_backward(
        True, info_self, query_s, key_s, value_s, attn_s, logs_s, grad_os
    )
    dk_s = (dk_s.astype(F32) + swap(dk_ss, "dp", 1, dp).astype(F32)).astype(LOW)
    dv_s = (dv_s.astype(F32) + swap(dv_ss, "dp", 1, dp).astype(F32)).astype(LOW)
    d_x = send_rows(
        (grad_r1 + dot_nn(dq_s, wq) + dot_nn(dk_s, wk) + dot_nn(dv_s, wv)).astype(LOW)
    ).astype(F32)
    d_qkv = reduce_grads(place, [(dq_s, x_own), (dk_s, x_own), (dv_s, x_own)], (4, 2))

    return (
        out,
        d_x,
        d_mem,
        jnp.swapaxes(d_qkv, 1, 2),
        d_mid[0],
        d_mid[1].T,
        jnp.swapaxes(d_mid[2:4], 1, 2),
        d_mid[4],
        d_up[0].T,
        d_down[0],
        sums[0:3],
        sums[3:6],
    )


def solution(mesh):
    rows = P(None, "dp", "tensor", None)
    in_specs = (
        P(None, "dp", None, None),
        P(None, "dp", None, None),
        rows,
        P(None, "dp"),
        P(None, "dp"),
        P(None, None, "tensor"),
        P("tensor", None),
        P(None, "tensor"),
        P(None, None, "tensor"),
        P("tensor", None),
        P(None, "tensor"),
        P("tensor", None),
        P(),
        P(),
    )
    out_specs = (
        rows,
        rows,
        rows,
        P(None, None, "tensor"),
        P("tensor", None),
        P(None, "tensor"),
        P(None, None, "tensor"),
        P("tensor", None),
        P(None, "tensor"),
        P("tensor", None),
        P(),
        P(),
    )
    return jax.shard_map(local, mesh=mesh, in_specs=in_specs, out_specs=out_specs, check_vma=False)
```

time: 1400 us -> 534 us (0.38)
  waiting for transfers between devices: 915 us -> 212 us
  matrix products: 210 us -> 39 us
  Pallas kernels: 0 us -> 111 us
  starting transfers between devices: 3.37 us -> 81.6 us
  other arithmetic: 100 us -> 47.7 us
  blocking collectives: 43 us -> 0 us
  local copies, waits for them, and re-layouts: 73.9 us -> 32.3 us
  loops' own time: 26 us -> 0 us
  between operations: 16.8 us -> 2.42 us
    reduce_scatter x14 -> x0, waiting for transfers between devices: 574 us -> none  [the longest x2 115 us: sequence(): lax.psum_scatter(dot_nn(hidden_low, ffn_out), 'tensor', scatter_dimension...]
    ppermute x0 -> x80, waiting for transfers between devices: none -> 212 us  [the longest x69 193 us: swap(): return lax.ppermute(value, axis, [(d, d ^ bit) for d in range(size)])]
    all_gather x10 -> x0, waiting for transfers between devices: 198 us -> none  [the longest x2 62.2 us: sequence(): lax.all_gather(grad_res3.astype(jnp.bfloat16), 'tensor', axis=0, tiled=True)]
    psum x1 -> x0, waiting for transfers between devices: 143 us -> none  [reduce_weights(): lax.psum((grads[0], grads[1], grads[2], grads[3], grads[4], grads[5], gra...]
    dot_general x76 -> x5, matrix products: 140 us -> 4.06 us  [dot_nn(): lax.dot_general(left, right, (((1,), (0,)), ((), ())), preferred_element_...]
    pallas_call x0 -> x7, Pallas kernels: none -> 111 us  [the longest x2 44.6 us: attend_backward(): pl.pallas_call(kernel, out_shape=(jax.ShapeDtypeStruct((rows, width), LOW...]
    ppermute x0 -> x80, starting transfers between devices: none -> 81.6 us  [the longest x69 66.5 us: swap(): return lax.ppermute(value, axis, [(d, d ^ bit) for d in range(size)])]
    reduce_sum x27 -> x0, other arithmetic: 44 us -> none  [the longest x9 19.9 us: norm_rows(): center = resid - jnp.mean(resid, -1, keepdims=True)]
  transfers between devices with their start and end apart: 25 -> 80, of which waited for: 23 -> 32; matrix products, arithmetic and copies ran while one was open for 20% -> 14% of each run, Pallas kernels for 0% -> 6%
where the time goes in v1:
time: 534 us; the launch traced here: 526 us
  waiting for transfers between devices  212 us (40%)
  Pallas kernels  111 us (21%)
  starting transfers between devices  81.6 us (15%)
  other arithmetic  47.7 us (9%)
  matrix products  39 us (7%)
  local copies, waits for them, and re-layouts  32.3 us (6%)
    ppermute x69, waiting for transfers between devices, swap(): return lax.ppermute(value, axis, [(d, d ^ bit) for d in range(size)])  193 us
    ppermute x69, starting transfers between devices, swap(): return lax.ppermute(value, axis, [(d, d ^ bit) for d in range(size)])  66.5 us
    pallas_call x2, Pallas kernels, attend_backward(): pl.pallas_call(kernel, out_shape=(jax.ShapeDtypeStruct((rows, width), LOW...  44.6 us
    pallas_call x1, Pallas kernels, middle(): pl.pallas_call(kernel, grid=(rows // block,), out_shape=(low_row, low_bro...  33.1 us
    pallas_call x2, Pallas kernels, attend_forward(): pl.pallas_call(kernel, out_shape=(jax.ShapeDtypeStruct((rows, width), LOW...  27.8 us
    dot_general x20, matrix products, dot_tn(): lax.dot_general(left, right, (((0,), (0,)), ((), ())), preferred_element_...  26.1 us
    ppermute x6, waiting for transfers between devices, send_rows(): lax.ppermute(lax.dynamic_slice_in_dim(value, (call + micro) % 2 * block,...  19.2 us
    unnamed x130, local copies, waits for them, and re-layouts  18.7 us
  transfers between devices with their start and end apart: 80, of which 32 were waited for; matrix products, arithmetic and copies ran while one was open for 14% of the time, Pallas kernels for 6%

profile of v1, /device:TPU:0, one launch (start us, length us, event | category | flops | bytes accessed | tf_op | source)
XLA Modules:
  0.0 526.2 jit_solution(14234447212429560468)
XLA Ops:
  2.2 5.0 collective-permute-start.4
  11.6 3.8 collective-permute-start.25
  17.0 2.8 dynamic-slice_bitcast_fusion.1
  24.8 3.8 collective-permute-start.19
  32.2 4.6 collective-permute-done.23
  36.8 3.9 collective-permute-start.10
  40.7 5.9 %collective-permute-done.18 = bf16[1,192,384]{2,1,0:T(8,128)(2,1)S(1)} collective-permute-done((bf16[1,192,384]{2,1,0:T(8,128)(2,1)S(1)}, bf16[1,192,384]{2,1,0:T(8,128)(2,1)S(1)}, u32[]{:S(2)}, u32[]{:S(2)}) %collective-permute-start.18) | collective-permute-done | bytes 147488 | tf_op jit(solution)/shard_map/ppermute | solution.py:354
  46.6 2.6 collective-permute-start.8
  49.3 13.2 %collective-permute-done.10 = bf16[5,48,384]{2,1,0:T(8,128)(2,1)S(1)} collective-permute-done((bf16[5,48,384]{2,1,0:T(8,128)(2,1)S(1)}, bf16[5,48,384]{2,1,0:T(8,128)(2,1)S(1)}, u32[]{:S(2)}, u32[]{:S(2)}) %collective-permute-start.10) | collective-permute-done | bytes 184352 | tf_op jit(solution)/shard_map/ppermute | solution.py:354
  63.9 12.8 %collective-permute-done.9 = bf16[5,48,384]{2,1,0:T(8,128)(2,1)S(1)} collective-permute-done((bf16[5,48,384]{2,1,0:T(8,128)(2,1)S(1)}, bf16[5,48,384]{2,1,0:T(8,128)(2,1)S(1)}, u32[]{:S(2)}, u32[]{:S(2)}) %collective-permute-start.9) | collective-permute-done | bytes 184352 | tf_op jit(solution)/shard_map/ppermute | solution.py:354
  76.7 2.1 collective-permute-start.1
  83.6 6.1 %collective-permute-done.5 = bf16[3,3,48,384]{3,2,0,1:T(8,128)(2,1)S(1)} collective-permute-done((bf16[3,3,48,384]{3,2,0,1:T(8,128)(2,1)S(1)}, bf16[3,3,48,384]{3,2,0,1:T(8,128)(2,1)S(1)}, u32[]{:S(2)}, u32[]{:S(2)}) %collective-permute-start.5) | collective-permute-done | bytes 331808 | tf_op jit(solution)/shard_map/ppermute | solution.py:354
  91.3 2.4 collective-permute-done.26
  95.4 2.0 collective-permute-done.20
  99.1 6.4 %collective-permute-done.11 = bf16[5,3,48,384]{3,2,0,1:T(8,128)(2,1)S(1)} collective-permute-done((bf16[5,3,48,384]{3,2,0,1:T(8,128)(2,1)S(1)}, bf16[5,3,48,384]{3,2,0,1:T(8,128)(2,1)S(1)}, u32[]{:S(2)}, u32[]{:S(2)}) %collective-permute-start.11) | collective-permute-done | bytes 552992 | tf_op jit(solution)/shard_map/ppermute | solution.py:354
  107.3 12.5 %collective-permute-done.6 = bf16[3,3,96,384]{3,2,0,1:T(8,128)(2,1)S(1)} collective-permute-done((bf16[3,3,96,384]{3,2,0,1:T(8,128)(2,1)S(1)}, bf16[3,3,96,384]{3,2,0,1:T(8,128)(2,1)S(1)}, u32[]{:S(2)}, u32[]{:S(2)}) %collective-permute-start.6) | collective-permute-done | bytes 663584 | tf_op jit(solution)/shard_map/ppermute | solution.py:354
  123.1 13.6 %collective-permute-done.21 = bf16[1,3,384,384]{3,2,1,0:T(8,128)(2,1)S(1)} collective-permute-done((bf16[1,3,384,384]{3,2,1,0:T(8,128)(2,1)S(1)}, bf16[1,3,384,384]{3,2,1,0:T(8,128)(2,1)S(1)}, u32[]{:S(2)}, u32[]{:S(2)}) %collective-permute-start.21) | collective-permute-done | bytes 884768 | tf_op jit(solution)/shard_map/ppermute | solution.py:354
  150.1 2.6 convolution_convert_fusion.4.v_ref
  152.6 13.1 %shard_map.229 = (bf16[512,768]{1,0:T(8,128)(2,1)S(1)}, f32[512,768]{1,0:T(8,128)S(1)}) custom-call(s32[2]{0:T(128)S(1)} %pad_add_fusion.1.info_ref, bf16[512,768]{1,0:T(8,128)(2,1)S(1)} %convolution_convert_fusion.6.q_ref, bf16[1024,768]{1,0:T(8,128)(2,1)S(1)} %convolution_convert_fusion.5.k_ref, bf16[1024,768]{1,0:T(8,128)(2,1)} %convolution_convert_fusion.4.v_ref), custom_call_target="tpu_custom_call" | custom-call | flops 4026531840 | bytes 10485760 | tf_op jit(solution)/shard_map/pallas_call | solution.py:91
  165.8 2.7 broadcast_select_fusion.3
  168.5 2.4 maximum_maximum_fusion.2
  170.9 2.1 broadcast_select_fusion.5
  173.1 2.4 maximum_maximum_fusion.1
  175.5 2.7 broadcast_select_fusion.1
  180.3 2.6 convolution_convert_fusion.2.v_ref
  184.3 2.9 shard_map.230
  188.3 14.6 %shard_map.231 = (bf16[512,768]{1,0:T(8,128)(2,1)S(1)}, f32[512,768]{1,0:T(8,128)S(1)}) custom-call(s32[2]{0:T(128)S(1)} %pad_add_fusion.2.info_ref, bf16[512,768]{1,0:T(8,128)(2,1)S(1)} %get-tuple-element.45.q_ref, bf16[1024,768]{1,0:T(8,128)(2,1)S(1)} %convolution_convert_fusion.3.k_ref, bf16[1024,768]{1,0:T(8,128)(2,1)} %convolution_convert_fusion.2.v_ref), custom_call_target="tpu_custom_call" | custom-call | flops 6442450944 | bytes 10485760 | tf_op jit(solution)/shard_map/pallas_call | solution.py:91
  205.0 33.1 %shard_map.232 = (bf16[512,768]{1,0:T(8,128)(2,1)S(1)}, bf16[512,3072]{1,0:T(8,128)(2,1)}, bf16[512,3072]{1,0:T(8,128)(2,1)}, bf16[512,768]{1,0:T(8,128)(2,1)S(1...) custom-call(f32[512,768]{1,0:T(8,128)} %copy-done, ...), custom_call_target="tpu_custom_call" | custom-call | flops 10871635968 | bytes 25165824 | tf_op jit(solution)/shard_map/pallas_call | solution.py:295
  241.0 24.2 %shard_map.233 = (bf16[512,768]{1,0:T(8,128)(2,1)S(1)}, bf16[512,768]{1,0:T(8,128)(2,1)S(1)}, bf16[512,768]{1,0:T(8,128)(2,1)S(1)}, bf16[512,768]{1,0:T(8,128)(2,1)S(1)}, bf16[512,768]{1,0:T(8,128)(2,1)S(1)}) custom-call(s32[2]{0:T(128)S(1)} %pad_add_fusion.2.info_ref, bf16[512,768]{1,0:T(8,128)(2,1)S(1)} %copy-done.13, bf16[1024,768]{1,0:T(8,128)(2,1)} %copy-done.17, ...), custom_call_target="tpu_custom_call" | custom-call | flops 16106127360 | bytes 10485760 | tf_op jit(solution)/shard_map/pallas_call | solution.py:170
  266.0 2.7 shard_map.234
  272.9 3.3 convolution_convert_fusion.1
  276.1 4.1 fusion.8
  280.2 3.3 convolution_convert_fusion
  283.5 4.0 fusion.5
  287.5 20.5 %shard_map.235 = (bf16[512,768]{1,0:T(8,128)(2,1)S(1)}, bf16[512,768]{1,0:T(8,128)(2,1)S(1)}, bf16[512,768]{1,0:T(8,128)(2,1)S(1)}, bf16[512,768]{1,0:T(8,128)(2,1)S(1)}, bf16[512,768]{1,0:T(8,128)(2,1)S(1)}) custom-call(s32[2]{0:T(128)S(1)} %pad_add_fusion.1.info_ref, bf16[512,768]{1,0:T(8,128)(2,1)S(1)} %copy-done.15, bf16[1024,768]{1,0:T(8,128)(2,1)} %copy-done.16, ...), custom_call_target="tpu_custom_call" | custom-call | flops 10066329600 | bytes 10485760 | tf_op jit(solution)/shard_map/pallas_call | solution.py:170
  309.8 5.5 %collective-permute-start.30 = (bf16[256,768]{1,0:T(8,128)(2,1)S(1)}, bf16[256,768]{1,0:T(8,128)(2,1)S(1)}, u32[]{:S(2)}, u32[]{:S(2)}) collective-permute-start(bf16[256,768]{1,0:T(8,128)(2,1)S(1)} %get-tuple-element.166), channel_id=1, source_target_pairs={{0,3},{4,2},{1,7},{5,6},{2,0},{6,1},{3,4},{7,5},{8,11},{12,10},{9,... | collective-permute-start | bytes 1179656 | tf_op jit(solution)/shard_map/ppermute | solution.py:468
  320.2 2.2 collective-permute-done.76
  322.8 3.4 collective-permute-done.77
  327.2 4.5 collective-permute-done.78
  332.7 3.8 collective-permute-done.79
  356.1 7.1 %collective-permute-done.34 = bf16[256,768]{1,0:T(8,128)(2,1)S(1)} collective-permute-done((bf16[256,768]{1,0:T(8,128)(2,1)S(1)}, bf16[256,768]{1,0:T(8,128)(2,1)S(1)}, u32[]{:S(2)}, u32[]{:S(2)}) %collective-permute-start.34) | collective-permute-done | bytes 393248 | tf_op jit(solution)/shard_map/ppermute | solution.py:468
  365.7 2.0 maximum_add_fusion
  370.6 12.0 %collective-permute-done.38 = bf16[256,768]{1,0:T(8,128)(2,1)S(1)} collective-permute-done((bf16[256,768]{1,0:T(8,128)(2,1)S(1)}, bf16[256,768]{1,0:T(8,128)(2,1)S(1)}, u32[]{:S(2)}, u32[]{:S(2)}) %collective-permute-start.38) | collective-permute-done | bytes 393248 | tf_op jit(solution)/shard_map/ppermute | solution.py:468
  385.2 5.2 collective-permute-done.40
  393.6 22.1 %collective-permute-done.58 = bf16[1,4,384,384]{3,2,1,0:T(8,128)(2,1)S(1)} collective-permute-done((bf16[1,4,384,384]{3,2,1,0:T(8,128)(2,1)S(1)}, bf16[1,4,384,384]{3,2,1,0:T(8,128)(2,1)S(1)}, u32[]{:S(2)}, u32[]{:S(2)}) %collective-permute-start.58) | collective-permute-done | bytes 1179680 | tf_op jit(solution)/shard_map/ppermute | solution.py:354
  419.0 2.8 collective-permute-start.44
  422.4 4.8 collective-permute-done.44
  427.2 3.5 collective-permute-done.43
  433.1 3.7 collective-permute-done.45
  437.5 2.4 collective-permute-start.71
  441.2 7.2 %collective-permute-done.69 = bf16[1,192,384]{2,1,0:T(8,128)(2,1)S(1)} collective-permute-done((bf16[1,192,384]{2,1,0:T(8,128)(2,1)S(1)}, bf16[1,192,384]{2,1,0:T(8,128)(2,1)S(1)}, u32[]{:S(2)}, u32[]{:S(2)}) %collective-permute-start.69) | collective-permute-done | bytes 147488 | tf_op jit(solution)/shard_map/ppermute | solution.py:354
  448.5 2.0 collective-permute-start.62
  450.5 6.3 %collective-permute-done.70 = bf16[1,192,384]{2,1,0:T(8,128)(2,1)S(1)} collective-permute-done((bf16[1,192,384]{2,1,0:T(8,128)(2,1)S(1)}, bf16[1,192,384]{2,1,0:T(8,128)(2,1)S(1)}, u32[]{:S(2)}, u32[]{:S(2)}) %collective-permute-start.70) | collective-permute-done | bytes 147488 | tf_op jit(solution)/shard_map/ppermute | solution.py:354
  456.9 1.8 collective-permute-start.72
  458.8 5.1 collective-permute-done.61
  464.6 3.5 collective-permute-done.49
  471.7 15.1 %collective-permute-done.50 = bf16[5,4,48,384]{3,2,0,1:T(8,128)(2,1)S(1)} collective-permute-done((bf16[5,4,48,384]{3,2,0,1:T(8,128)(2,1)S(1)}, bf16[5,4,48,384]{3,2,0,1:T(8,128)(2,1)S(1)}, u32[]{:S(2)}, u32[]{:S(2)}) %collective-permute-start.50) | collective-permute-done | bytes 737312 | tf_op jit(solution)/shard_map/ppermute | solution.py:354
  488.8 1.8 collective-permute-start.52
  490.8 4.5 collective-permute-done.51
  495.3 4.7 collective-permute-done.52
  500.6 5.1 collective-permute-done.54
  507.6 5.9 %collective-permute-done.55 = bf16[5,96,384]{2,1,0:T(8,128)(2,1)S(1)} collective-permute-done((bf16[5,96,384]{2,1,0:T(8,128)(2,1)S(1)}, bf16[5,96,384]{2,1,0:T(8,128)(2,1)S(1)}, u32[]{:S(2)}, u32[]{:S(2)}) %collective-permute-start.55) | collective-permute-done | bytes 368672 | tf_op jit(solution)/shard_map/ppermute | solution.py:354
  517.5 2.0 copy.66
  519.5 2.8 maximum_convert_fusion
  (389 shorter events, 124.1 us)
Async XLA Ops:
  2.2 21.3 %collective-permute-start.4 = (bf16[3,48,384]{2,1,0:T(8,128)(2,1)}, bf16[3,48,384]{2,1,0:T(8,128)(2,1)S(1)}, u32[]{:S(2)}, u32[]{:S(2)}) collective-permute-start(bf16[3,48,384]{2,1,0:T(8,128)(2,1)} %dynamic-slice_bitcast_fusion.6), channel_id=1, source_target_pairs={{0,3},{1,2},{2,1},{3,0},{4,7},{5,6},{6,5},{7,4},{8,11},{9,10},{10,... | collective-permute-start | bytes 331784 | tf_op jit(solution)/shard_map/ppermute | solution.py:354
  7.3 17.5 %collective-permute-start.3 = (bf16[3,48,384]{2,1,0:T(8,128)(2,1)}, bf16[3,48,384]{2,1,0:T(8,128)(2,1)S(1)}, u32[]{:S(2)}, u32[]{:S(2)}) collective-permute-start(bf16[3,48,384]{2,1,0:T(8,128)(2,1)} %dynamic-slice_bitcast_fusion.6), channel_id=1, source_target_pairs={{0,2},{1,3},{2,0},{3,1},{4,6},{5,7},{6,4},{7,5},{8,10},{9,11},{10,... | collective-permute-start | bytes 331784 | tf_op jit(solution)/shard_map/ppermute | solution.py:354
  7.3 21.3 %collective-permute-start.2 = (bf16[3,48,384]{2,1,0:T(8,128)(2,1)}, bf16[3,48,384]{2,1,0:T(8,128)(2,1)S(1)}, u32[]{:S(2)}, u32[]{:S(2)}) collective-permute-start(bf16[3,48,384]{2,1,0:T(8,128)(2,1)} %dynamic-slice_bitcast_fusion.6), channel_id=1, source_target_pairs={{0,1},{1,0},{2,3},{3,2},{4,5},{5,4},{6,7},{7,6},{8,9},{9,8},{10,11... | collective-permute-start | bytes 331784 | tf_op jit(solution)/shard_map/ppermute | solution.py:354
  8.7 14.1 %collective-permute-start = (s32[2]{0:T(128)S(1)}, s32[2]{0:T(128)S(1)}, u32[]{:S(2)}, u32[]{:S(2)}) collective-permute-start(s32[2]{0:T(128)S(1)} %fusion.45), channel_id=1, source_target_pairs={{0,4},{2,6},{5,1},{7,3},{8,12},{10,14},{13,9},{15,11},{16,20},{18,... | collective-permute-start | bytes 32 | tf_op jit(solution)/shard_map/ppermute | solution.py:455
  11.6 17.0 %collective-permute-start.25 = (bf16[1,192,384]{2,1,0:T(8,128)(2,1)}, bf16[1,192,384]{2,1,0:T(8,128)(2,1)S(1)}, u32[]{:S(2)}, u32[]{:S(2)}) collective-permute-start(bf16[1,192,384]{2,1,0:T(8,128)(2,1)} %dynamic-slice_bitcast_fusion.4), channel_id=1, source_target_pairs={{0,3},{1,2},{2,1},{3,0},{4,7},{5,6},{6,5},{7,4},{8,11},{9,10},{10,... | collective-permute-start | bytes 442376 | tf_op jit(solution)/shard_map/ppermute | solution.py:354
  22.8 8.7 %collective-permute-start.24 = (bf16[1,192,384]{2,1,0:T(8,128)(2,1)}, bf16[1,192,384]{2,1,0:T(8,128)(2,1)S(1)}, u32[]{:S(2)}, u32[]{:S(2)}) collective-permute-start(bf16[1,192,384]{2,1,0:T(8,128)(2,1)} %dynamic-slice_bitcast_fusion.4), channel_id=1, source_target_pairs={{0,2},{1,3},{2,0},{3,1},{4,6},{5,7},{6,4},{7,5},{8,10},{9,11},{10,... | collective-permute-start | bytes 442376 | tf_op jit(solution)/shard_map/ppermute | solution.py:354
  23.5 13.3 %collective-permute-start.23 = (bf16[1,192,384]{2,1,0:T(8,128)(2,1)}, bf16[1,192,384]{2,1,0:T(8,128)(2,1)S(1)}, u32[]{:S(2)}, u32[]{:S(2)}) collective-permute-start(bf16[1,192,384]{2,1,0:T(8,128)(2,1)} %dynamic-slice_bitcast_fusion.4), channel_id=1, source_target_pairs={{0,1},{1,0},{2,3},{3,2},{4,5},{5,4},{6,7},{7,6},{8,9},{9,8},{10,11... | collective-permute-start | bytes 442376 | tf_op jit(solution)/shard_map/ppermute | solution.py:354
  24.8 12.0 %collective-permute-start.19 = (bf16[1,192,384]{2,1,0:T(8,128)(2,1)S(1)}, bf16[1,192,384]{2,1,0:T(8,128)(2,1)S(1)}, u32[]{:S(2)}, u32[]{:S(2)}) collective-permute-start(bf16[1,192,384]{2,1,0:T(8,128)(2,1)S(1)} %dynamic-slice_bitcast_fusion.5), channel_id=1, source_target_pairs={{0,3},{1,2},{2,1},{3,0},{4,7},{5,6},{6,5},{7,4},{8,11},{9,10},{10,... | collective-permute-start | bytes 442376 | tf_op jit(solution)/shard_map/ppermute | solution.py:354
  28.6 18.0 %collective-permute-start.18 = (bf16[1,192,384]{2,1,0:T(8,128)(2,1)S(1)}, bf16[1,192,384]{2,1,0:T(8,128)(2,1)S(1)}, u32[]{:S(2)}, u32[]{:S(2)}) collective-permute-start(bf16[1,192,384]{2,1,0:T(8,128)(2,1)S(1)} %dynamic-slice_bitcast_fusion.5), channel_id=1, source_target_pairs={{0,2},{1,3},{2,0},{3,1},{4,6},{5,7},{6,4},{7,5},{8,10},{9,11},{10,... | collective-permute-start | bytes 442376 | tf_op jit(solution)/shard_map/ppermute | solution.py:354
  28.6 18.0 %collective-permute-start.17 = (bf16[1,192,384]{2,1,0:T(8,128)(2,1)S(1)}, bf16[1,192,384]{2,1,0:T(8,128)(2,1)S(1)}, u32[]{:S(2)}, u32[]{:S(2)}) collective-permute-start(bf16[1,192,384]{2,1,0:T(8,128)(2,1)S(1)} %dynamic-slice_bitcast_fusion.5), channel_id=1, source_target_pairs={{0,1},{1,0},{2,3},{3,2},{4,5},{5,4},{6,7},{7,6},{8,9},{9,8},{10,11... | collective-permute-start | bytes 442376 | tf_op jit(solution)/shard_map/ppermute | solution.py:354
  31.5 49.0 %collective-permute-start.15 = (bf16[256,768]{1,0:T(8,128)(2,1)S(1)}, bf16[256,768]{1,0:T(8,128)(2,1)S(1)}, u32[]{:S(2)}, u32[]{:S(2)}) collective-permute-start(bf16[256,768]{1,0:T(8,128)(2,1)S(1)} %get-tuple-element.169), channel_id=1, source_target_pairs={{0,0},{1,4},{4,1},{5,5},{3,2},{2,6},{7,3},{6,7},{8,8},{9,12},{12,9... | collective-permute-start | bytes 1179656 | tf_op jit(solution)/shard_map/ppermute | solution.py:478
  36.8 45.3 %collective-permute-start.16 = (bf16[256,768]{1,0:T(8,128)(2,1)S(1)}, bf16[256,768]{1,0:T(8,128)(2,1)S(1)}, u32[]{:S(2)}, u32[]{:S(2)}) collective-permute-start(bf16[256,768]{1,0:T(8,128)(2,1)S(1)} %get-tuple-element.170), channel_id=1, source_target_pairs={{3,0},{2,4},{7,1},{6,5},{0,2},{1,6},{4,3},{5,7},{11,8},{10,12},{15... | collective-permute-start | bytes 1179656 | tf_op jit(solution)/shard_map/ppermute | solution.py:478
  36.8 25.7 %collective-permute-start.10 = (bf16[5,48,384]{2,1,0:T(8,128)(2,1)S(1)}, bf16[5,48,384]{2,1,0:T(8,128)(2,1)S(1)}, u32[]{:S(2)}, u32[]{:S(2)}) collective-permute-start(bf16[5,48,384]{2,1,0:T(8,128)(2,1)S(1)} %constant_dynamic-slice_fusion.8), channel_id=1, source_target_pairs={{0,3},{1,2},{2,1},{3,0},{4,7},{5,6},{6,5},{7,4},{8,11},{9,10},{10,... | collective-permute-start | bytes 552968 | tf_op jit(solution)/shard_map/ppermute | solution.py:354
  46.6 30.1 %collective-permute-start.9 = (bf16[5,48,384]{2,1,0:T(8,128)(2,1)S(1)}, bf16[5,48,384]{2,1,0:T(8,128)(2,1)S(1)}, u32[]{:S(2)}, u32[]{:S(2)}) collective-permute-start(bf16[5,48,384]{2,1,0:T(8,128)(2,1)S(1)} %constant_dynamic-slice_fusion.8), channel_id=1, source_target_pairs={{0,2},{1,3},{2,0},{3,1},{4,6},{5,7},{6,4},{7,5},{8,10},{9,11},{10,... | collective-permute-start | bytes 552968 | tf_op jit(solution)/shard_map/ppermute | solution.py:354
  46.6 32.2 %collective-permute-start.8 = (bf16[5,48,384]{2,1,0:T(8,128)(2,1)S(1)}, bf16[5,48,384]{2,1,0:T(8,128)(2,1)S(1)}, u32[]{:S(2)}, u32[]{:S(2)}) collective-permute-start(bf16[5,48,384]{2,1,0:T(8,128)(2,1)S(1)} %constant_dynamic-slice_fusion.8), channel_id=1, source_target_pairs={{0,1},{1,0},{2,3},{3,2},{4,5},{5,4},{6,7},{7,6},{8,9},{9,8},{10,11... | collective-permute-start | bytes 552968 | tf_op jit(solution)/shard_map/ppermute | solution.py:354
  62.5 75.9 %collective-permute-start.14 = (bf16[1024,768]{1,0:T(8,128)(2,1)S(1)}, bf16[1024,768]{1,0:T(8,128)(2,1)S(1)}, u32[]{:S(2)}, u32[]{:S(2)}) collective-permute-start(bf16[1024,768]{1,0:T(8,128)(2,1)S(1)} %copy-done.36), channel_id=1, source_target_pairs={{0,4},{2,6},{5,1},{7,3},{8,12},{10,14},{13,9},{15,11},{16,20},{18,... | collective-permute-start | bytes 4718600 | tf_op jit(solution)/shard_map/ppermute | solution.py:455
  76.7 64.0 %collective-permute-start.1 = (bf16[1024,768]{1,0:T(8,128)(2,1)S(1)}, bf16[1024,768]{1,0:T(8,128)(2,1)S(1)}, u32[]{:S(2)}, u32[]{:S(2)}) collective-permute-start(bf16[1024,768]{1,0:T(8,128)(2,1)S(1)} %copy-done.35), channel_id=1, source_target_pairs={{0,4},{2,6},{5,1},{7,3},{8,12},{10,14},{13,9},{15,11},{16,20},{18,... | collective-permute-start | bytes 4718600 | tf_op jit(solution)/shard_map/ppermute | solution.py:455
  78.9 10.8 %collective-permute-start.5 = (bf16[3,3,48,384]{3,2,0,1:T(8,128)(2,1)S(1)}, bf16[3,3,48,384]{3,2,0,1:T(8,128)(2,1)S(1)}, u32[]{:S(2)}, u32[]{:S(2)}) collective-permute-start(bf16[3,3,48,384]{3,2,0,1:T(8,128)(2,1)S(1)} %pad_maximum_fusion.20), channel_id=1, source_target_pairs={{0,16},{4,20},{8,24},{12,28},{16,0},{20,4},{24,8},{28,12},{1,17},{... | collective-permute-start | bytes 995336 | tf_op jit(solution)/shard_map/ppermute | solution.py:354
  80.5 13.2 %collective-permute-start.26 = (bf16[1,3,192,384]{3,2,1,0:T(8,128)(2,1)S(1)}, bf16[1,3,192,384]{3,2,1,0:T(8,128)(2,1)S(1)}, u32[]{:S(2)}, u32[]{:S(2)}) collective-permute-start(bf16[1,3,192,384]{3,2,1,0:T(8,128)(2,1)S(1)} %pad_maximum_fusion.17), channel_id=1, source_target_pairs={{0,8},{4,12},{8,0},{12,4},{16,24},{20,28},{24,16},{28,20},{1,9},{5... | collective-permute-start | bytes 1327112 | tf_op jit(solution)/shard_map/ppermute | solution.py:354
  82.1 15.3 %collective-permute-start.20 = (bf16[1,3,192,384]{3,2,1,0:T(8,128)(2,1)S(1)}, bf16[1,3,192,384]{3,2,1,0:T(8,128)(2,1)S(1)}, u32[]{:S(2)}, u32[]{:S(2)}) collective-permute-start(bf16[1,3,192,384]{3,2,1,0:T(8,128)(2,1)S(1)} %pad_maximum_fusion.16), channel_id=1, source_target_pairs={{0,16},{4,20},{8,24},{12,28},{16,0},{20,4},{24,8},{28,12},{1,17},{... | collective-permute-start | bytes 1327112 | tf_op jit(solution)/shard_map/ppermute | solution.py:354
  89.7 15.9 %collective-permute-start.11 = (bf16[5,3,48,384]{3,2,0,1:T(8,128)(2,1)S(1)}, bf16[5,3,48,384]{3,2,0,1:T(8,128)(2,1)S(1)}, u32[]{:S(2)}, u32[]{:S(2)}) collective-permute-start(bf16[5,3,48,384]{3,2,0,1:T(8,128)(2,1)S(1)} %pad_maximum_fusion.15), channel_id=1, source_target_pairs={{0,8},{4,12},{8,0},{12,4},{16,24},{20,28},{24,16},{28,20},{1,9},{5... | collective-permute-start | bytes 1658888 | tf_op jit(solution)/shard_map/ppermute | solution.py:354
  93.7 26.1 %collective-permute-start.6 = (bf16[3,3,96,384]{3,2,0,1:T(8,128)(2,1)S(1)}, bf16[3,3,96,384]{3,2,0,1:T(8,128)(2,1)S(1)}, u32[]{:S(2)}, u32[]{:S(2)}) collective-permute-start(bf16[3,3,96,384]{3,2,0,1:T(8,128)(2,1)S(1)} %pad_maximum_fusion.12), channel_id=1, source_target_pairs={{0,8},{4,12},{8,0},{12,4},{16,24},{20,28},{24,16},{28,20},{1,9},{5... | collective-permute-start | bytes 1990664 | tf_op jit(solution)/shard_map/ppermute | solution.py:354
  97.4 23.9 %collective-permute-start.27 = (bf16[1,3,384,384]{3,2,1,0:T(8,128)(2,1)S(1)}, bf16[1,3,384,384]{3,2,1,0:T(8,128)(2,1)S(1)}, u32[]{:S(2)}, u32[]{:S(2)}) collective-permute-start(bf16[1,3,384,384]{3,2,1,0:T(8,128)(2,1)S(1)} %pad_maximum_fusion.9), channel_id=1, source_target_pairs={{0,16},{4,20},{8,24},{12,28},{16,0},{20,4},{24,8},{28,12},{1,17},{... | collective-permute-start | bytes 2654216 | tf_op jit(solution)/shard_map/ppermute | solution.py:354
  105.6 31.2 %collective-permute-start.21 = (bf16[1,3,384,384]{3,2,1,0:T(8,128)(2,1)S(1)}, bf16[1,3,384,384]{3,2,1,0:T(8,128)(2,1)S(1)}, u32[]{:S(2)}, u32[]{:S(2)}) collective-permute-start(bf16[1,3,384,384]{3,2,1,0:T(8,128)(2,1)S(1)} %pad_maximum_fusion.8), channel_id=1, source_target_pairs={{0,8},{4,12},{8,0},{12,4},{16,24},{20,28},{24,16},{28,20},{1,9},{5... | collective-permute-start | bytes 2654216 | tf_op jit(solution)/shard_map/ppermute | solution.py:354
  119.8 23.9 %collective-permute-start.12 = (bf16[5,3,96,384]{3,2,0,1:T(8,128)(2,1)S(1)}, bf16[5,3,96,384]{3,2,0,1:T(8,128)(2,1)S(1)}, u32[]{:S(2)}, u32[]{:S(2)}) collective-permute-start(bf16[5,3,96,384]{3,2,0,1:T(8,128)(2,1)S(1)} %pad_maximum_fusion.6), channel_id=1, source_target_pairs={{0,16},{4,20},{8,24},{12,28},{16,0},{20,4},{24,8},{28,12},{1,17},{... | collective-permute-start | bytes 3317768 | tf_op jit(solution)/shard_map/ppermute | solution.py:354
  121.3 24.9 %collective-permute-start.7 = (bf16[3,3,192,384]{3,2,0,1:T(8,128)(2,1)S(1)}, bf16[3,3,192,384]{3,2,0,1:T(8,128)(2,1)S(1)}, u32[]{:S(2)}, u32[]{:S(2)}) collective-permute-start(bf16[3,3,192,384]{3,2,0,1:T(8,128)(2,1)S(1)} %pad_maximum_fusion.5), channel_id=1, source_target_pairs={{0,4},{4,0},{8,12},{12,8},{16,20},{20,16},{24,28},{28,24},{1,5},{5... | collective-permute-start | bytes 3981320 | tf_op jit(solution)/shard_map/ppermute | solution.py:354
  136.7 29.1 %collective-permute-start.28 = (bf16[1,3,768,384]{3,2,1,0:T(8,128)(2,1)}, bf16[1,3,768,384]{3,2,1,0:T(8,128)(2,1)}, u32[]{:S(2)}, u32[]{:S(2)}) collective-permute-start(bf16[1,3,768,384]{3,2,1,0:T(8,128)(2,1)} %pad_maximum_fusion.2), channel_id=1, source_target_pairs={{0,4},{4,0},{8,12},{12,8},{16,20},{20,16},{24,28},{28,24},{1,5},{5... | collective-permute-start | bytes 5308424 | tf_op jit(solution)/shard_map/ppermute | solution.py:354
  138.4 32.5 %collective-permute-start.22 = (bf16[1,3,768,384]{3,2,1,0:T(8,128)(2,1)}, bf16[1,3,768,384]{3,2,1,0:T(8,128)(2,1)}, u32[]{:S(2)}, u32[]{:S(2)}) collective-permute-start(bf16[1,3,768,384]{3,2,1,0:T(8,128)(2,1)} %pad_maximum_fusion.1), channel_id=1, source_target_pairs={{0,4},{4,0},{8,12},{12,8},{16,20},{20,16},{24,28},{28,24},{1,5},{5... | collective-permute-start | bytes 5308424 | tf_op jit(solution)/shard_map/ppermute | solution.py:354
  145.8 29.7 %collective-permute-start.13 = (bf16[5,3,192,384]{3,2,0,1:T(8,128)(2,1)}, bf16[5,3,192,384]{3,2,0,1:T(8,128)(2,1)}, u32[]{:S(2)}, u32[]{:S(2)}) collective-permute-start(bf16[5,3,192,384]{3,2,0,1:T(8,128)(2,1)} %pad_maximum_fusion), channel_id=1, source_target_pairs={{0,4},{4,0},{8,12},{12,8},{16,20},{20,16},{24,28},{28,24},{1,5},{5... | collective-permute-start | bytes 6635528 | tf_op jit(solution)/shard_map/ppermute | solution.py:354
  287.5 31.0 %collective-permute-start.75 = (f32[8,768]{1,0:T(8,128)S(1)}, f32[8,768]{1,0:T(8,128)S(1)}, u32[]{:S(2)}, u32[]{:S(2)}) collective-permute-start(f32[8,768]{1,0:T(8,128)S(1)} %add.328), channel_id=1, source_target_pairs={{0,4},{4,0},{8,12},{12,8},{16,20},{20,16},{24,28},{28,24},{1,5},{5... | collective-permute-start | bytes 73736 | tf_op jit(solution)/shard_map/ppermute | solution.py:354
  308.9 28.2 %collective-permute-start.29 = (bf16[256,768]{1,0:T(8,128)(2,1)S(1)}, bf16[256,768]{1,0:T(8,128)(2,1)S(1)}, u32[]{:S(2)}, u32[]{:S(2)}) collective-permute-start(bf16[256,768]{1,0:T(8,128)(2,1)S(1)} %get-tuple-element.165), channel_id=1, source_target_pairs={{0,0},{4,1},{1,4},{5,5},{2,3},{6,2},{3,7},{7,6},{8,8},{12,9},{9,12... | collective-permute-start | bytes 1179656 | tf_op jit(solution)/shard_map/ppermute | solution.py:468
  309.8 27.9 %collective-permute-start.30 = (bf16[256,768]{1,0:T(8,128)(2,1)S(1)}, bf16[256,768]{1,0:T(8,128)(2,1)S(1)}, u32[]{:S(2)}, u32[]{:S(2)}) collective-permute-start(bf16[256,768]{1,0:T(8,128)(2,1)S(1)} %get-tuple-element.166), channel_id=1, source_target_pairs={{0,3},{4,2},{1,7},{5,6},{2,0},{6,1},{3,4},{7,5},{8,11},{12,10},{9,... | collective-permute-start | bytes 1179656 | tf_op jit(solution)/shard_map/ppermute | solution.py:468
  317.7 21.0 %collective-permute-start.31 = (bf16[512,768]{1,0:T(8,128)(2,1)S(1)}, bf16[512,768]{1,0:T(8,128)(2,1)S(1)}, u32[]{:S(2)}, u32[]{:S(2)}) collective-permute-start(bf16[512,768]{1,0:T(8,128)(2,1)S(1)} %get-tuple-element.58), channel_id=1, source_target_pairs={{0,4},{4,0},{8,12},{12,8},{16,20},{20,16},{24,28},{28,24},{1,5},{5... | collective-permute-start | bytes 2359304 | tf_op jit(solution)/shard_map/ppermute | solution.py:354
  318.5 21.6 %collective-permute-start.32 = (bf16[512,768]{1,0:T(8,128)(2,1)S(1)}, bf16[512,768]{1,0:T(8,128)(2,1)S(1)}, u32[]{:S(2)}, u32[]{:S(2)}) collective-permute-start(bf16[512,768]{1,0:T(8,128)(2,1)S(1)} %get-tuple-element.60), channel_id=1, source_target_pairs={{0,4},{4,0},{8,12},{12,8},{16,20},{20,16},{24,28},{28,24},{1,5},{5... | collective-permute-start | bytes 2359304 | tf_op jit(solution)/shard_map/ppermute | solution.py:354
  337.6 25.8 %collective-permute-start.66 = (bf16[1,4,768,384]{3,2,1,0:T(8,128)(2,1)S(1)}, bf16[1,4,768,384]{3,2,1,0:T(8,128)(2,1)S(1)}, u32[]{:S(2)}, u32[]{:S(2)}) collective-permute-start(bf16[1,4,768,384]{3,2,1,0:T(8,128)(2,1)S(1)} %bitcast.321), channel_id=1, source_target_pairs={{0,4},{4,0},{8,12},{12,8},{16,20},{20,16},{24,28},{28,24},{1,5},{5... | collective-permute-start | bytes 7077896 | tf_op jit(solution)/shard_map/ppermute | solution.py:354
  338.7 29.1 %collective-permute-start.57 = (bf16[1,4,768,384]{3,2,1,0:T(8,128)(2,1)}, bf16[1,4,768,384]{3,2,1,0:T(8,128)(2,1)S(1)}, u32[]{:S(2)}, u32[]{:S(2)}) collective-permute-start(bf16[1,4,768,384]{3,2,1,0:T(8,128)(2,1)} %bitcast.100), channel_id=1, source_target_pairs={{0,4},{4,0},{8,12},{12,8},{16,20},{20,16},{24,28},{28,24},{1,5},{5... | collective-permute-start | bytes 7077896 | tf_op jit(solution)/shard_map/ppermute | solution.py:354
  341.4 14.0 %collective-permute-start.33 = (bf16[256,768]{1,0:T(8,128)(2,1)S(1)}, bf16[256,768]{1,0:T(8,128)(2,1)S(1)}, u32[]{:S(2)}, u32[]{:S(2)}) collective-permute-start(bf16[256,768]{1,0:T(8,128)(2,1)S(1)} %get-tuple-element.161), channel_id=1, source_target_pairs={{0,0},{4,1},{1,4},{5,5},{2,3},{6,2},{3,7},{7,6},{8,8},{12,9},{9,12... | collective-permute-start | bytes 1179656 | tf_op jit(solution)/shard_map/ppermute | solution.py:468
  342.3 20.9 %collective-permute-start.34 = (bf16[256,768]{1,0:T(8,128)(2,1)S(1)}, bf16[256,768]{1,0:T(8,128)(2,1)S(1)}, u32[]{:S(2)}, u32[]{:S(2)}) collective-permute-start(bf16[256,768]{1,0:T(8,128)(2,1)S(1)} %get-tuple-element.162), channel_id=1, source_target_pairs={{0,3},{4,2},{1,7},{5,6},{2,0},{6,1},{3,4},{7,5},{8,11},{12,10},{9,... | collective-permute-start | bytes 1179656 | tf_op jit(solution)/shard_map/ppermute | solution.py:468
  347.6 16.4 %collective-permute-start.39 = (bf16[3,4,192,384]{3,2,0,1:T(8,128)(2,1)S(1)}, bf16[3,4,192,384]{3,2,0,1:T(8,128)(2,1)S(1)}, u32[]{:S(2)}, u32[]{:S(2)}) collective-permute-start(bf16[3,4,192,384]{3,2,0,1:T(8,128)(2,1)S(1)} %pad_maximum_fusion.3), channel_id=1, source_target_pairs={{0,4},{4,0},{8,12},{12,8},{16,20},{20,16},{24,28},{28,24},{1,5},{5... | collective-permute-start | bytes 5308424 | tf_op jit(solution)/shard_map/ppermute | solution.py:354
  355.4 13.7 %collective-permute-start.37 = (bf16[256,768]{1,0:T(8,128)(2,1)S(1)}, bf16[256,768]{1,0:T(8,128)(2,1)S(1)}, u32[]{:S(2)}, u32[]{:S(2)}) collective-permute-start(bf16[256,768]{1,0:T(8,128)(2,1)S(1)} %get-tuple-element.157), channel_id=1, source_target_pairs={{0,0},{4,1},{1,4},{5,5},{2,3},{6,2},{3,7},{7,6},{8,8},{12,9},{9,12... | collective-permute-start | bytes 1179656 | tf_op jit(solution)/shard_map/ppermute | solution.py:468
  363.2 19.4 %collective-permute-start.38 = (bf16[256,768]{1,0:T(8,128)(2,1)S(1)}, bf16[256,768]{1,0:T(8,128)(2,1)S(1)}, u32[]{:S(2)}, u32[]{:S(2)}) collective-permute-start(bf16[256,768]{1,0:T(8,128)(2,1)S(1)} %get-tuple-element.158), channel_id=1, source_target_pairs={{0,3},{4,2},{1,7},{5,6},{2,0},{6,1},{3,4},{7,5},{8,11},{12,10},{9,... | collective-permute-start | bytes 1179656 | tf_op jit(solution)/shard_map/ppermute | solution.py:468
  363.4 58.3 %collective-permute-start.48 = (bf16[5,4,192,384]{3,2,0,1:T(8,128)(2,1)}, bf16[5,4,192,384]{3,2,0,1:T(8,128)(2,1)S(1)}, u32[]{:S(2)}, u32[]{:S(2)}) collective-permute-start(bf16[5,4,192,384]{3,2,0,1:T(8,128)(2,1)} %constant_dynamic-update-slice_fusion.5), channel_id=1, source_target_pairs={{0,4},{4,0},{8,12},{12,8},{16,20},{20,16},{24,28},{28,24},{1,5},{5... | collective-permute-start | bytes 8847368 | tf_op jit(solution)/shard_map/ppermute | solution.py:354
  364.1 28.8 %collective-permute-start.67 = (bf16[1,4,384,384]{3,2,1,0:T(8,128)(2,1)S(1)}, bf16[1,4,384,384]{3,2,1,0:T(8,128)(2,1)S(1)}, u32[]{:S(2)}, u32[]{:S(2)}) collective-permute-start(bf16[1,4,384,384]{3,2,1,0:T(8,128)(2,1)S(1)} %dynamic-slice_convert_fusion.1), channel_id=1, source_target_pairs={{0,8},{4,12},{8,0},{12,4},{16,24},{20,28},{24,16},{28,20},{1,9},{5... | collective-permute-start | bytes 3538952 | tf_op jit(solution)/shard_map/ppermute | solution.py:354
  367.8 22.6 %collective-permute-start.40 = (bf16[3,4,96,384]{3,2,0,1:T(8,128)(2,1)S(1)}, bf16[3,4,96,384]{3,2,0,1:T(8,128)(2,1)S(1)}, u32[]{:S(2)}, u32[]{:S(2)}) collective-permute-start(bf16[3,4,96,384]{3,2,0,1:T(8,128)(2,1)S(1)} %dynamic-slice_convert_fusion.3), channel_id=1, source_target_pairs={{0,16},{4,20},{8,24},{12,28},{16,0},{20,4},{24,8},{28,12},{1,17},{... | collective-permute-start | bytes 2654216 | tf_op jit(solution)/shard_map/ppermute | solution.py:354
  369.0 46.6 %collective-permute-start.58 = (bf16[1,4,384,384]{3,2,1,0:T(8,128)(2,1)S(1)}, bf16[1,4,384,384]{3,2,1,0:T(8,128)(2,1)S(1)}, u32[]{:S(2)}, u32[]{:S(2)}) collective-permute-start(bf16[1,4,384,384]{3,2,1,0:T(8,128)(2,1)S(1)} %dynamic-slice_convert_fusion.2), channel_id=1, source_target_pairs={{0,16},{4,20},{8,24},{12,28},{16,0},{20,4},{24,8},{28,12},{1,17},{... | collective-permute-start | bytes 3538952 | tf_op jit(solution)/shard_map/ppermute | solution.py:354
  390.7 26.5 %collective-permute-start.41 = (bf16[3,4,48,384]{3,2,0,1:T(8,128)(2,1)S(1)}, bf16[3,4,48,384]{3,2,0,1:T(8,128)(2,1)S(1)}, u32[]{:S(2)}, u32[]{:S(2)}) collective-permute-start(bf16[3,4,48,384]{3,2,0,1:T(8,128)(2,1)S(1)} %dynamic-slice_convert_fusion.7), channel_id=1, source_target_pairs={{0,8},{4,12},{8,0},{12,4},{16,24},{20,28},{24,16},{28,20},{1,9},{5... | collective-permute-start | bytes 1327112 | tf_op jit(solution)/shard_map/ppermute | solution.py:354
  393.3 44.0 %collective-permute-start.68 = (bf16[1,4,192,384]{3,2,1,0:T(8,128)(2,1)S(1)}, bf16[1,4,192,384]{3,2,1,0:T(8,128)(2,1)S(1)}, u32[]{:S(2)}, u32[]{:S(2)}) collective-permute-start(bf16[1,4,192,384]{3,2,1,0:T(8,128)(2,1)S(1)} %dynamic-slice_convert_fusion.5), channel_id=1, source_target_pairs={{0,16},{4,20},{8,24},{12,28},{16,0},{20,4},{24,8},{28,12},{1,17},{... | collective-permute-start | bytes 1769480 | tf_op jit(solution)/shard_map/ppermute | solution.py:354
  416.0 24.0 %collective-permute-start.59 = (bf16[1,4,192,384]{3,2,1,0:T(8,128)(2,1)S(1)}, bf16[1,4,192,384]{3,2,1,0:T(8,128)(2,1)S(1)}, u32[]{:S(2)}, u32[]{:S(2)}) collective-permute-start(bf16[1,4,192,384]{3,2,1,0:T(8,128)(2,1)S(1)} %dynamic-slice_convert_fusion.6), channel_id=1, source_target_pairs={{0,8},{4,12},{8,0},{12,4},{16,24},{20,28},{24,16},{28,20},{1,9},{5... | collective-permute-start | bytes 1769480 | tf_op jit(solution)/shard_map/ppermute | solution.py:354
  421.7 8.9 %collective-permute-start.43 = (bf16[3,48,384]{2,1,0:T(8,128)(2,1)S(1)}, bf16[3,48,384]{2,1,0:T(8,128)(2,1)S(1)}, u32[]{:S(2)}, u32[]{:S(2)}) collective-permute-start(bf16[3,48,384]{2,1,0:T(8,128)(2,1)S(1)} %get-tuple-element.192), channel_id=1, source_target_pairs={{0,2},{1,3},{2,0},{3,1},{4,6},{5,7},{6,4},{7,5},{8,10},{9,11},{10,... | collective-permute-start | bytes 331784 | tf_op jit(solution)/shard_map/ppermute | solution.py:354
  431.4 36.7 %collective-permute-start.49 = (bf16[5,4,96,384]{3,2,0,1:T(8,128)(2,1)S(1)}, bf16[5,4,96,384]{3,2,0,1:T(8,128)(2,1)S(1)}, u32[]{:S(2)}, u32[]{:S(2)}) collective-permute-start(bf16[5,4,96,384]{3,2,0,1:T(8,128)(2,1)S(1)} %dynamic-slice_convert_fusion), channel_id=1, source_target_pairs={{0,8},{4,12},{8,0},{12,4},{16,24},{20,28},{24,16},{28,20},{1,9},{5... | collective-permute-start | bytes 4423688 | tf_op jit(solution)/shard_map/ppermute | solution.py:354
  436.9 27.6 %collective-permute-start.46 = (bf16[3,96,384]{2,1,0:T(8,128)(2,1)S(1)}, bf16[3,96,384]{2,1,0:T(8,128)(2,1)S(1)}, u32[]{:S(2)}, u32[]{:S(2)}) collective-permute-start(bf16[3,96,384]{2,1,0:T(8,128)(2,1)S(1)} %pad_maximum_fusion.24), channel_id=1, source_target_pairs={{0,16},{4,20},{8,24},{12,28},{16,0},{20,4},{24,8},{28,12},{1,17},{... | collective-permute-start | bytes 663560 | tf_op jit(solution)/shard_map/ppermute | solution.py:354
  437.4 11.0 %collective-permute-start.69 = (bf16[1,192,384]{2,1,0:T(8,128)(2,1)S(1)}, bf16[1,192,384]{2,1,0:T(8,128)(2,1)S(1)}, u32[]{:S(2)}, u32[]{:S(2)}) collective-permute-start(bf16[1,192,384]{2,1,0:T(8,128)(2,1)S(1)} %get-tuple-element.180), channel_id=1, source_target_pairs={{0,1},{1,0},{2,3},{3,2},{4,5},{5,4},{6,7},{7,6},{8,9},{9,8},{10,11... | collective-permute-start | bytes 442376 | tf_op jit(solution)/shard_map/ppermute | solution.py:354
  437.5 10.9 %collective-permute-start.71 = (bf16[1,192,384]{2,1,0:T(8,128)(2,1)S(1)}, bf16[1,192,384]{2,1,0:T(8,128)(2,1)S(1)}, u32[]{:S(2)}, u32[]{:S(2)}) collective-permute-start(bf16[1,192,384]{2,1,0:T(8,128)(2,1)S(1)} %get-tuple-element.181), channel_id=1, source_target_pairs={{0,3},{1,2},{2,1},{3,0},{4,7},{5,6},{6,5},{7,4},{8,11},{9,10},{10,... | collective-permute-start | bytes 442376 | tf_op jit(solution)/shard_map/ppermute | solution.py:354
  439.9 16.9 %collective-permute-start.70 = (bf16[1,192,384]{2,1,0:T(8,128)(2,1)S(1)}, bf16[1,192,384]{2,1,0:T(8,128)(2,1)S(1)}, u32[]{:S(2)}, u32[]{:S(2)}) collective-permute-start(bf16[1,192,384]{2,1,0:T(8,128)(2,1)S(1)} %get-tuple-element.182), channel_id=1, source_target_pairs={{0,2},{1,3},{2,0},{3,1},{4,6},{5,7},{6,4},{7,5},{8,10},{9,11},{10,... | collective-permute-start | bytes 442376 | tf_op jit(solution)/shard_map/ppermute | solution.py:354
  448.5 8.5 %collective-permute-start.60 = (bf16[1,192,384]{2,1,0:T(8,128)(2,1)S(1)}, bf16[1,192,384]{2,1,0:T(8,128)(2,1)S(1)}, u32[]{:S(2)}, u32[]{:S(2)}) collective-permute-start(bf16[1,192,384]{2,1,0:T(8,128)(2,1)S(1)} %get-tuple-element.185), channel_id=1, source_target_pairs={{0,1},{1,0},{2,3},{3,2},{4,5},{5,4},{6,7},{7,6},{8,9},{9,8},{10,11... | collective-permute-start | bytes 442376 | tf_op jit(solution)/shard_map/ppermute | solution.py:354
  448.5 10.3 %collective-permute-start.62 = (bf16[1,192,384]{2,1,0:T(8,128)(2,1)S(1)}, bf16[1,192,384]{2,1,0:T(8,128)(2,1)S(1)}, u32[]{:S(2)}, u32[]{:S(2)}) collective-permute-start(bf16[1,192,384]{2,1,0:T(8,128)(2,1)S(1)} %get-tuple-element.186), channel_id=1, source_target_pairs={{0,3},{1,2},{2,1},{3,0},{4,7},{5,6},{6,5},{7,4},{8,11},{9,10},{10,... | collective-permute-start | bytes 442376 | tf_op jit(solution)/shard_map/ppermute | solution.py:354
  456.9 12.1 %collective-permute-start.72 = (bf16[1,192,384]{2,1,0:T(8,128)(2,1)S(1)}, bf16[1,192,384]{2,1,0:T(8,128)(2,1)S(1)}, u32[]{:S(2)}, u32[]{:S(2)}) collective-permute-start(bf16[1,192,384]{2,1,0:T(8,128)(2,1)S(1)} %fusion.26), channel_id=1, source_target_pairs={{0,16},{4,20},{8,24},{12,28},{16,0},{20,4},{24,8},{28,12},{1,17},{... | collective-permute-start | bytes 442376 | tf_op jit(solution)/shard_map/ppermute | solution.py:354
  468.5 18.3 %collective-permute-start.50 = (bf16[5,4,48,384]{3,2,0,1:T(8,128)(2,1)S(1)}, bf16[5,4,48,384]{3,2,0,1:T(8,128)(2,1)S(1)}, u32[]{:S(2)}, u32[]{:S(2)}) collective-permute-start(bf16[5,4,48,384]{3,2,0,1:T(8,128)(2,1)S(1)} %dynamic-slice_convert_fusion.4), channel_id=1, source_target_pairs={{0,16},{4,20},{8,24},{12,28},{16,0},{20,4},{24,8},{28,12},{1,17},{... | collective-permute-start | bytes 2211848 | tf_op jit(solution)/shard_map/ppermute | solution.py:354
  468.9 38.5 %collective-permute-start.47 = (bf16[3,192,384]{2,1,0:T(8,128)(2,1)S(1)}, bf16[3,192,384]{2,1,0:T(8,128)(2,1)S(1)}, u32[]{:S(2)}, u32[]{:S(2)}) collective-permute-start(bf16[3,192,384]{2,1,0:T(8,128)(2,1)S(1)} %pad_maximum_fusion.18), channel_id=1, source_target_pairs={{0,4},{4,0},{8,12},{12,8},{16,20},{20,16},{24,28},{28,24},{1,5},{5... | collective-permute-start | bytes 1327112 | tf_op jit(solution)/shard_map/ppermute | solution.py:354
  469.1 19.7 %collective-permute-start.73 = (bf16[1,384,384]{2,1,0:T(8,128)(2,1)S(1)}, bf16[1,384,384]{2,1,0:T(8,128)(2,1)S(1)}, u32[]{:S(2)}, u32[]{:S(2)}) collective-permute-start(bf16[1,384,384]{2,1,0:T(8,128)(2,1)S(1)} %pad_maximum_fusion.23), channel_id=1, source_target_pairs={{0,8},{4,12},{8,0},{12,4},{16,24},{20,28},{24,16},{28,20},{1,9},{5... | collective-permute-start | bytes 884744 | tf_op jit(solution)/shard_map/ppermute | solution.py:354
  469.9 30.7 %collective-permute-start.64 = (bf16[1,384,384]{2,1,0:T(8,128)(2,1)S(1)}, bf16[1,384,384]{2,1,0:T(8,128)(2,1)S(1)}, u32[]{:S(2)}, u32[]{:S(2)}) collective-permute-start(bf16[1,384,384]{2,1,0:T(8,128)(2,1)S(1)} %pad_maximum_fusion.22), channel_id=1, source_target_pairs={{0,16},{4,20},{8,24},{12,28},{16,0},{20,4},{24,8},{28,12},{1,17},{... | collective-permute-start | bytes 884744 | tf_op jit(solution)/shard_map/ppermute | solution.py:354
  488.8 11.2 %collective-permute-start.52 = (bf16[5,48,384]{2,1,0:T(8,128)(2,1)S(1)}, bf16[5,48,384]{2,1,0:T(8,128)(2,1)S(1)}, u32[]{:S(2)}, u32[]{:S(2)}) collective-permute-start(bf16[5,48,384]{2,1,0:T(8,128)(2,1)S(1)} %get-tuple-element.175), channel_id=1, source_target_pairs={{0,2},{1,3},{2,0},{3,1},{4,6},{5,7},{6,4},{7,5},{8,10},{9,11},{10,... | collective-permute-start | bytes 552968 | tf_op jit(solution)/shard_map/ppermute | solution.py:354
  495.3 20.6 %collective-permute-start.74 = (bf16[1,768,384]{2,1,0:T(8,128)(2,1)S(1)}, bf16[1,768,384]{2,1,0:T(8,128)(2,1)S(1)}, u32[]{:S(2)}, u32[]{:S(2)}) collective-permute-start(bf16[1,768,384]{2,1,0:T(8,128)(2,1)S(1)} %pad_maximum_fusion.14), channel_id=1, source_target_pairs={{0,4},{4,0},{8,12},{12,8},{16,20},{20,16},{24,28},{28,24},{1,5},{5... | collective-permute-start | bytes 1769480 | tf_op jit(solution)/shard_map/ppermute | solution.py:354
  507.3 8.6 %collective-permute-start.65 = (bf16[1,768,384]{2,1,0:T(8,128)(2,1)S(1)}, bf16[1,768,384]{2,1,0:T(8,128)(2,1)S(1)}, u32[]{:S(2)}, u32[]{:S(2)}) collective-permute-start(bf16[1,768,384]{2,1,0:T(8,128)(2,1)S(1)} %pad_maximum_fusion.13), channel_id=1, source_target_pairs={{0,4},{4,0},{8,12},{12,8},{16,20},{20,16},{24,28},{28,24},{1,5},{5... | collective-permute-start | bytes 1769480 | tf_op jit(solution)/shard_map/ppermute | solution.py:354
  (76 other events, 541.8 us)
